TPU v7x, 32 devices: a whole 2x2x4 slice. The times are simulated.
32 devices in a mesh: batch: 4 (over x, core), seq: 8 (over z, y).
Axes of the slice: x: 2, y: 2, z: 4, core: 2. Of those that a mesh axis runs over, the one named last changes fastest.
Arguments:
- tokens: bfloat16 [16, 2048, 1024], P('batch', 'seq'), may hold values from -6 to 6
- segments: int32 [16, 2048], P('batch', 'seq'), may hold values from 0 to 40, as said below
- cotangent: bfloat16 [16, 2048, 1024], P('batch', 'seq'), may hold values from -6 to 6
- first_gain: bfloat16 [1024], P(('batch', 'seq')), may hold values from 0.5 to 1.5
- query_weight: bfloat16 [1024, 1024], P(('batch', 'seq')), may hold values from -0.1875 to 0.1875
- key_weight: bfloat16 [1024, 128], P(('batch', 'seq')), may hold values from -0.1875 to 0.1875
- value_weight: bfloat16 [1024, 128], P(('batch', 'seq')), may hold values from -0.1875 to 0.1875
- out_weight: bfloat16 [1024, 1024], P(None, ('batch', 'seq')), may hold values from -1 to 1
- second_gain: bfloat16 [1024], P(('batch', 'seq')), may hold values from 0.5 to 1.5
- gate_weight: bfloat16 [1024, 3072], P(('batch', 'seq')), may hold values from -0.1875 to 0.1875
- up_weight: bfloat16 [1024, 3072], P(('batch', 'seq')), may hold values from -0.1875 to 0.1875
- down_weight: bfloat16 [3072, 1024], P(None, ('batch', 'seq')), may hold values from -0.109375 to 0.109375
Outputs:
- output: bfloat16 [16, 2048, 1024], P('batch', 'seq')
- grad_input: bfloat16 [16, 2048, 1024], P('batch', 'seq')
- grad_first_gain: float32 [1024], P(('batch', 'seq'))
- grad_query_weight: float32 [1024, 1024], P(('batch', 'seq'))
- grad_key_weight: float32 [1024, 128], P(('batch', 'seq'))
- grad_value_weight: float32 [1024, 128], P(('batch', 'seq'))
- grad_out_weight: float32 [1024, 1024], P(None, ('batch', 'seq'))
- grad_second_gain: float32 [1024], P(('batch', 'seq'))
- grad_gate_weight: float32 [1024, 3072], P(('batch', 'seq'))
- grad_up_weight: float32 [1024, 3072], P(('batch', 'seq'))
- grad_down_weight: float32 [3072, 1024], P(None, ('batch', 'seq'))
Inputs may be any that keep to these rules, and one draw needn't show every extreme that they name: `segments`: each row is 0 at its first position and rises by 0 or 1 from one position to the next; among the 4 rows of each index of batch, one row is 0 throughout, and some other row reaches the largest value.
All inputs are finite; a program needn't handle non-finite values.
Results may differ from a plain program's by a relative error of at most 0.014.
Values may be sent and summed in bfloat16 or wider, within the bound.
A program may use at most 256 MiB of HBM per device.

v0:
```python
import jax
import jax.numpy as jnp
from jax import lax
from jax.sharding import PartitionSpec as P

WINDOW = 1024
MICRO = 2


def prefix(value, axis, join, neutral):
    count, mine = (lax.axis_size(axis), lax.axis_index(axis))
    pieces = jax.tree.map(lambda part: lax.all_gather(part, axis), value)
    subtotal = jax.tree.map(
        lambda part, zero: jnp.full_like(part, 0) + jnp.asarray(zero, part.dtype), value, neutral
    )

    def step(position, subtotal):
        longer = join(subtotal, jax.tree.map(lambda part: part[position], pieces))
        return jax.tree.map(lambda new, old: jnp.where(position < mine, new, old), longer, subtotal)

    return lax.fori_loop(0, count - 1, step, subtotal)


def shifted(value, axis, steps):
    count = lax.axis_size(axis)
    initial, last = (max(0, -steps), min(count, count - steps))
    return lax.ppermute(value, axis, [(source, source + steps) for source in range(initial, last)])


def rms_scale(values, gain):
    return values * lax.rsqrt(jnp.mean(values * values, axis=-1, keepdims=True) + 1e-06) * gain


def rotate(values, cosine, sine):
    half_width = values.shape[-1] // 2
    turned = jnp.concatenate([-values[..., half_width:], values[..., :half_width]], axis=-1)
    return values * cosine + turned * sine


def tables(positions, head_dim):
    inverse = 10000.0 ** (-2.0 * jnp.arange(head_dim // 2, dtype=jnp.float32) / head_dim)
    inverse = jnp.concatenate([inverse, inverse])
    angle = positions.astype(jnp.float32)[:, None] * inverse[None, :]
    return (jnp.cos(angle), jnp.sin(angle))


def gated(gate, up_part):
    return jax.nn.gelu(gate, approximate=True) * up_part


def matmul(left, right):
    return jnp.dot(left, right, preferred_element_type=jnp.float32)


def left_times(left, right):
    return lax.dot_general(
        left, right, (((0,), (0,)), ((), ())), preferred_element_type=jnp.float32
    )


def right_times(left, right):
    return lax.dot_general(
        left, right, (((1,), (1,)), ((), ())), preferred_element_type=jnp.float32
    )


def allowed_pairs(query_place, key_place, starts):
    later = key_place[None, :] <= query_place[:, None]
    inside = query_place[:, None] - key_place[None, :] < WINDOW
    same_doc = key_place[None, :] >= starts[:, None]
    return later & inside & same_doc


def doc_starts(segments):
    seqs, block_len = segments.shape
    offset = lax.axis_index("seq") * block_len
    local = jnp.arange(block_len, dtype=jnp.int32)
    last_doc = segments[:, -1]
    first_of_last = (
        jnp.min(jnp.where(segments == last_doc[:, None], local[None, :], block_len), axis=1)
        + offset
    )

    def combine(earlier, later):
        empty = later[0] < 0
        same = later[0] == earlier[0]
        return (
            jnp.where(empty, earlier[0], later[0]),
            jnp.where(empty | same, earlier[1], later[1]),
        )

    identity = (jnp.full((seqs,), -1, jnp.int32), jnp.zeros((seqs,), jnp.int32))
    before_doc, before_start = prefix((last_doc, first_of_last), "seq", combine, identity)
    previous = jnp.concatenate([before_doc[:, None], segments[:, :-1]], axis=1)
    fresh = segments != previous
    marks = jnp.where(fresh, local[None, :] + offset, -1)
    marks = marks.at[:, 0].set(jnp.where(fresh[:, 0], offset, before_start))
    return (lax.cummax(marks, axis=1), local + offset)


def fetch_weights(
    first_gain,
    query_weight,
    key_weight,
    value_weight,
    out_weight,
    second_gain,
    gate_weight,
    up_weight,
    down_weight,
):
    return (
        lax.all_gather(first_gain, ("batch", "seq"), axis=0, tiled=True),
        lax.all_gather(query_weight, ("batch", "seq"), axis=0, tiled=True),
        lax.all_gather(key_weight, ("batch", "seq"), axis=0, tiled=True),
        lax.all_gather(value_weight, ("batch", "seq"), axis=0, tiled=True),
        lax.all_gather(out_weight, ("batch", "seq"), axis=1, tiled=True),
        lax.all_gather(second_gain, ("batch", "seq"), axis=0, tiled=True),
        lax.all_gather(gate_weight, ("batch", "seq"), axis=0, tiled=True),
        lax.all_gather(up_weight, ("batch", "seq"), axis=0, tiled=True),
        lax.all_gather(down_weight, ("batch", "seq"), axis=1, tiled=True),
    )


def attend_one(query, pairs, starts, query_place, key_place, scale, head_dim):
    keys = pairs[:, :head_dim]
    values = pairs[:, head_dim:]
    allowed = allowed_pairs(query_place, key_place, starts)
    score = jnp.einsum("qhd,kd->hqk", query, keys, preferred_element_type=jnp.float32) * scale
    score = jnp.where(allowed[None], score, -1e30)
    peak = jnp.max(score, axis=-1, keepdims=True)
    log_total = peak + jnp.log(jnp.sum(jnp.exp(score - peak), axis=-1, keepdims=True))
    weights_low = jnp.exp(score - log_total).astype(jnp.bfloat16)
    result = jnp.einsum("hqk,kd->qhd", weights_low, values, preferred_element_type=jnp.float32)
    return (result, log_total[..., 0])


def attend_back(query, pairs, starts, log_total, grad_out, query_place, key_place, scale, head_dim):
    keys = pairs[:, :head_dim]
    values = pairs[:, head_dim:]
    allowed = allowed_pairs(query_place, key_place, starts)
    score = jnp.einsum("qhd,kd->hqk", query, keys, preferred_element_type=jnp.float32) * scale
    score = jnp.where(allowed[None], score, -1e30)
    weights = jnp.exp(score - log_total[..., None])
    weights_low = weights.astype(jnp.bfloat16)
    grad_weights = jnp.einsum("qhd,kd->hqk", grad_out, values, preferred_element_type=jnp.float32)
    grad_values = jnp.einsum(
        "hqk,qhd->kd", weights_low, grad_out, preferred_element_type=jnp.float32
    )
    grad_score = (
        weights * (grad_weights - jnp.sum(weights * grad_weights, axis=-1, keepdims=True))
    ).astype(jnp.bfloat16)
    grad_query = (
        jnp.einsum("hqk,kd->qhd", grad_score, keys, preferred_element_type=jnp.float32) * scale
    )
    grad_keys = (
        jnp.einsum("hqk,qhd->kd", grad_score, query, preferred_element_type=jnp.float32) * scale
    )
    return (grad_query, jnp.concatenate([grad_keys, grad_values], axis=-1))


def on_device(
    tokens,
    segments,
    cotangent,
    first_gain,
    query_weight,
    key_weight,
    value_weight,
    out_weight,
    second_gain,
    gate_weight,
    up_weight,
    down_weight,
):
    seqs, block_len, width = tokens.shape
    head_dim = key_weight.shape[1]
    heads = query_weight.shape[1] // head_dim
    reach = (WINDOW - 1 + block_len - 1) // block_len
    span = (reach + 1) * block_len
    scale = head_dim ** (-0.5)
    per_batch = seqs // MICRO
    rows = per_batch * block_len
    starts, query_place = doc_starts(segments)
    key_place = query_place[0] - reach * block_len + jnp.arange(span, dtype=jnp.int32)
    cosine, sine = tables((query_place[None, :] - starts).reshape(-1), head_dim)

    def forward_item(item):
        return attend_one(item[0], item[1], item[2], query_place, key_place, scale, head_dim)

    def backward_item(item):
        return attend_back(
            item[0], item[1], item[2], item[3], item[4], query_place, key_place, scale, head_dim
        )

    outputs = []
    stash = []
    for batch_index in range(MICRO):
        lower = batch_index * per_batch
        weights_now = fetch_weights(
            first_gain,
            query_weight,
            key_weight,
            value_weight,
            out_weight,
            second_gain,
            gate_weight,
            up_weight,
            down_weight,
        )
        (
            gain_one,
            query_full,
            key_full,
            value_full,
            out_full,
            gain_two,
            gate_full,
            up_full,
            down_full,
        ) = weights_now
        inputs_part = tokens[lower : lower + per_batch].reshape(rows, width).astype(jnp.float32)
        cosine_part = cosine[lower * block_len : (lower + per_batch) * block_len]
        sine_part = sine[lower * block_len : (lower + per_batch) * block_len]
        normed_one = rms_scale(inputs_part, gain_one.astype(jnp.float32)).astype(jnp.bfloat16)
        query = rotate(
            matmul(normed_one, query_full).reshape(rows, heads, head_dim),
            cosine_part[:, None, :],
            sine_part[:, None, :],
        ).astype(jnp.bfloat16)
        key_rot = rotate(matmul(normed_one, key_full), cosine_part, sine_part).astype(jnp.bfloat16)
        value_low = matmul(normed_one, value_full).astype(jnp.bfloat16)
        own_pairs = jnp.concatenate([key_rot, value_low], axis=-1).reshape(
            per_batch, block_len, 2 * head_dim
        )
        pieces = []
        for distance in range(reach, 0, -1):
            pieces.append(shifted(own_pairs, "seq", distance))
        window_pairs = jnp.concatenate(pieces + [own_pairs], axis=1)
        query_seq = query.reshape(per_batch, block_len, heads, head_dim)
        attended, log_total = lax.map(
            forward_item, (query_seq, window_pairs, starts[lower : lower + per_batch])
        )
        attended_low = attended.reshape(rows, heads * head_dim).astype(jnp.bfloat16)
        mixed = inputs_part + matmul(attended_low, out_full)
        normed_two = rms_scale(mixed, gain_two.astype(jnp.float32)).astype(jnp.bfloat16)
        gate = matmul(normed_two, gate_full)
        up_part = matmul(normed_two, up_full)
        hidden = gated(gate, up_part).astype(jnp.bfloat16)
        result = mixed + matmul(hidden, down_full)
        outputs.append(result.astype(jnp.bfloat16).reshape(per_batch, block_len, width))
        stash.append(
            (
                normed_one,
                query_seq,
                window_pairs,
                log_total,
                attended_low,
                mixed,
                normed_two,
                gate,
                up_part,
                hidden,
            )
        )
    grad_inputs = []
    sums = None
    for batch_index in range(MICRO):
        lower = batch_index * per_batch
        weights_now = fetch_weights(
            first_gain,
            query_weight,
            key_weight,
            value_weight,
            out_weight,
            second_gain,
            gate_weight,
            up_weight,
            down_weight,
        )
        (
            gain_one,
            query_full,
            key_full,
            value_full,
            out_full,
            gain_two,
            gate_full,
            up_full,
            down_full,
        ) = weights_now
        (
            normed_one,
            query_seq,
            window_pairs,
            log_total,
            attended_low,
            mixed,
            normed_two,
            gate,
            up_part,
            hidden,
        ) = stash[batch_index]
        inputs_part = tokens[lower : lower + per_batch].reshape(rows, width).astype(jnp.float32)
        cosine_part = cosine[lower * block_len : (lower + per_batch) * block_len]
        sine_part = sine[lower * block_len : (lower + per_batch) * block_len]
        grad_rows = cotangent[lower : lower + per_batch].reshape(rows, width)
        grad_down = left_times(hidden, grad_rows)
        grad_hidden = right_times(grad_rows, down_full)
        unused, pull_gated = jax.vjp(gated, gate, up_part)
        grad_gate, grad_up = pull_gated(grad_hidden)
        grad_gate = grad_gate.astype(jnp.bfloat16)
        grad_up = grad_up.astype(jnp.bfloat16)
        grad_gate_w = left_times(normed_two, grad_gate)
        grad_up_w = left_times(normed_two, grad_up)
        grad_normed_two = right_times(grad_gate, gate_full) + right_times(grad_up, up_full)
        unused, pull_second = jax.vjp(rms_scale, mixed, gain_two.astype(jnp.float32))
        grad_mixed, grad_gain_two = pull_second(grad_normed_two)
        grad_mixed = grad_mixed + grad_rows.astype(jnp.float32)
        grad_branch = grad_mixed.astype(jnp.bfloat16)
        grad_out_w = left_times(attended_low, grad_branch)
        grad_attended = right_times(grad_branch, out_full).astype(jnp.bfloat16)
        grad_query, grad_pairs = lax.map(
            backward_item,
            (
                query_seq,
                window_pairs,
                starts[lower : lower + per_batch],
                log_total,
                grad_attended.reshape(per_batch, block_len, heads, head_dim),
            ),
        )
        own_grad = grad_pairs[:, reach * block_len :]
        for distance in range(1, reach + 1):
            piece = grad_pairs[
                :, (reach - distance) * block_len : (reach - distance + 1) * block_len
            ]
            own_grad = own_grad + shifted(piece.astype(jnp.bfloat16), "seq", -distance).astype(
                piece.dtype
            )
        grad_key_rot = own_grad[..., :head_dim].reshape(rows, head_dim)
        grad_value = own_grad[..., head_dim:].reshape(rows, head_dim).astype(jnp.bfloat16)
        grad_q = (
            rotate(
                grad_query.reshape(rows, heads, head_dim),
                cosine_part[:, None, :],
                -sine_part[:, None, :],
            )
            .reshape(rows, heads * head_dim)
            .astype(jnp.bfloat16)
        )
        grad_k = rotate(grad_key_rot, cosine_part, -sine_part).astype(jnp.bfloat16)
        grad_query_w = left_times(normed_one, grad_q)
        grad_key_w = left_times(normed_one, grad_k)
        grad_value_w = left_times(normed_one, grad_value)
        grad_normed_one = (
            right_times(grad_q, query_full)
            + right_times(grad_k, key_full)
            + right_times(grad_value, value_full)
        )
        unused, pull_first = jax.vjp(rms_scale, inputs_part, gain_one.astype(jnp.float32))
        grad_x, grad_gain_one = pull_first(grad_normed_one)
        grad_x = grad_x + grad_mixed
        grad_inputs.append(grad_x.astype(jnp.bfloat16).reshape(per_batch, block_len, width))
        newest = (
            grad_gain_one,
            grad_query_w,
            grad_key_w,
            grad_value_w,
            grad_out_w,
            grad_gain_two,
            grad_gate_w,
            grad_up_w,
            grad_down,
        )
        sums = (
            newest if sums is None else tuple((older + newer for older, newer in zip(sums, newest)))
        )
    shares = (
        lax.psum_scatter(sums[0], ("batch", "seq"), scatter_dimension=0, tiled=True),
        lax.psum_scatter(sums[1], ("batch", "seq"), scatter_dimension=0, tiled=True),
        lax.psum_scatter(sums[2], ("batch", "seq"), scatter_dimension=0, tiled=True),
        lax.psum_scatter(sums[3], ("batch", "seq"), scatter_dimension=0, tiled=True),
        lax.psum_scatter(sums[4], ("batch", "seq"), scatter_dimension=1, tiled=True),
        lax.psum_scatter(sums[5], ("batch", "seq"), scatter_dimension=0, tiled=True),
        lax.psum_scatter(sums[6], ("batch", "seq"), scatter_dimension=0, tiled=True),
        lax.psum_scatter(sums[7], ("batch", "seq"), scatter_dimension=0, tiled=True),
        lax.psum_scatter(sums[8], ("batch", "seq"), scatter_dimension=1, tiled=True),
    )
    output = jnp.concatenate(outputs, axis=0)
    grad_input = jnp.concatenate(grad_inputs, axis=0)
    return (
        output,
        grad_input,
        shares[0],
        shares[1],
        shares[2],
        shares[3],
        shares[4],
        shares[5],
        shares[6],
        shares[7],
        shares[8],
    )


def solution(mesh):
    in_specs = (
        P("batch", "seq", None),
        P("batch", "seq"),
        P("batch", "seq", None),
        P(("batch", "seq")),
        P(("batch", "seq"), None),
        P(("batch", "seq"), None),
        P(("batch", "seq"), None),
        P(None, ("batch", "seq")),
        P(("batch", "seq")),
        P(("batch", "seq"), None),
        P(("batch", "seq"), None),
        P(None, ("batch", "seq")),
    )
    out_specs = (
        P("batch", "seq", None),
        P("batch", "seq", None),
        P(("batch", "seq")),
        P(("batch", "seq"), None),
        P(("batch", "seq"), None),
        P(("batch", "seq"), None),
        P(None, ("batch", "seq")),
        P(("batch", "seq")),
        P(("batch", "seq"), None),
        P(("batch", "seq"), None),
        P(None, ("batch", "seq")),
    )
    return jax.shard_map(
        on_device, mesh=mesh, in_specs=in_specs, out_specs=out_specs, check_vma=False
    )
```

profile of v0, /device:TPU:0, one launch (start us, length us, event | category | flops | bytes accessed | tf_op | source)
XLA Modules:
  0.0 1706.0 jit_solution(14736776529898938477)
XLA Ops:
  14.9 13.1 all-reduce.6
  34.0 39.4 %all-reduce.8 = (bf16[1024]{0:T(1024)(128)(2,1)S(1)}, bf16[1024]{0:T(1024)(128)(2,1)S(1)}) all-reduce(bf16[1024]{0:T(1024)(128)(2,1)S(1)} %dynamic-update-slice.3, bf16[1024]{0:T(1024)(128)(2,1)S(1)} %dynamic-update-slice.6), channel_id=1, replica_groups=mesh['batch'=4,'seq'=8] {'batch','seq'}, use_global_device_ids=true, to_apply=%add | all-reduce | flops 2048 | bytes 8192
  75.6 67.6 %all_gather.23 = bf16[1024,128]{1,0:T(8,128)(2,1)S(1)} all-gather(bf16[32,128]{1,0:T(8,128)(2,1)S(1)} %copy-done.96), channel_id=1, replica_groups=mesh['batch'=4,'seq'=8] {'batch','seq'}, dimensions={0}, use_global_device_ids=true | all-gather | bytes 270336 | tf_op jit(solution)/shard_map/all_gather | solution.py:115
  143.3 66.1 %all_gather.26 = bf16[1024,128]{1,0:T(8,128)(2,1)S(1)} all-gather(bf16[32,128]{1,0:T(8,128)(2,1)S(1)} %copy-done.97), channel_id=1, replica_groups=mesh['batch'=4,'seq'=8] {'batch','seq'}, dimensions={0}, use_global_device_ids=true | all-gather | bytes 270336 | tf_op jit(solution)/shard_map/all_gather | solution.py:116
  218.7 2.9 collective-permute-start.1
  223.6 3.8 collective-permute-start.3
  244.7 4.0 copy.227
  248.7 2.9 fusion.176
  254.5 16.6 while.69
  274.3 3.6 multiply_reduce_fusion.5
  283.1 8.0 fusion.177
  291.1 9.4 fusion.178
  300.5 53.7 %all-gather.16.cloned.1.call-done = bf16[3072,1024]{0,1:T(8,128)(2,1)} async-done(((bf16[3072,32]{0,1:T(8,128)(2,1)}), bf16[3072,1024]{0,1:T(8,128)(2,1)}) %all-gather.16.cloned.1.call-update) | async-done | bytes 6291472 | tf_op jit(solution)/shard_map/all_gather | solution.py:121
  354.2 13.8 multiply_convert_fusion.1
  368.1 7.9 fusion.183
  376.0 4.3 multiply_reduce_fusion.1
  387.6 42.2 %while.71 = (s32[]{:T(128)}, f32[2,256,8,128]{3,2,1,0:T(8,128)}, f32[2,1280,256]{2,1,0:T(8,128)}, bf16[2,1280,256]{2,1,0:T(8,128)(2,1)}, s32[2,256]{1,0:T(2,128)...) while((s32[]{:T(128)}, f32[2,256,8,128]{3,2,1,0:T(8,128)}, ...), condition=%wide.region_21.22_spmd.clone, body=%wide.region_19.21_spmd.clone.sunk | while | flops 3381755392 | bytes 128573672 | solution.py:323
  392.4 3.2 fusion.305
  403.4 3.4 fusion.307
  413.5 3.2 fusion.305
  424.5 3.4 fusion.307
  438.8 5.0 collective-permute-done.10
  443.8 17.8 %collective-permute-done.11 = bf16[2,256,256]{2,1,0:T(8,128)(2,1)S(1)} collective-permute-done((bf16[2,256,256]{2,1,0:T(8,128)(2,1)S(1)}, bf16[2,256,256]{2,1,0:T(8,128)(2,1)S(1)}, u32[]{:S(2)}, u32[]{:S(2)}) %collective-permute-start.11) | collective-permute-done | bytes 262176 | tf_op jit(solution)/shard_map/ppermute | solution.py:27
  469.2 12.7 collective-permute-start.4
  483.9 3.0 collective-permute-start.6
  503.2 16.6 while.70
  520.6 3.6 multiply_reduce_fusion.4
  524.6 9.4 fusion.182
  534.0 5.3 fusion.181
  539.4 11.7 multiply_convert_fusion
  551.0 7.8 fusion.185
  558.9 6.9 multiply_reduce_fusion
  573.1 42.4 %while.72 = (s32[]{:T(128)}, f32[2,256,8,128]{3,2,1,0:T(8,128)}, f32[2,1280,256]{2,1,0:T(8,128)}, bf16[2,1280,256]{2,1,0:T(8,128)(2,1)}, s32[2,256]{1,0:T(2,128)...) while((s32[]{:T(128)}, f32[2,256,8,128]{3,2,1,0:T(8,128)}, ...), condition=%wide.region_26.27_spmd.clone, body=%wide.region_24.26_spmd.clone.sunk | while | flops 3381755392 | bytes 128573672 | solution.py:323
  578.0 3.2 fusion.316
  589.0 3.4 fusion.318
  599.1 3.2 fusion.316
  610.2 3.4 fusion.318
  622.9 3.5 collective-permute-done.12
  626.4 10.8 collective-permute-done.13
  637.1 3.1 collective-permute-done.14
  640.2 21.3 %collective-permute-done.15 = bf16[2,256,256]{2,1,0:T(8,128)(2,1)S(1)} collective-permute-done((bf16[2,256,256]{2,1,0:T(8,128)(2,1)S(1)}, bf16[2,256,256]{2,1,0:T(8,128)(2,1)S(1)}, u32[]{:S(2)}, u32[]{:S(2)}) %collective-permute-start.15) | collective-permute-done | bytes 262176 | tf_op jit(solution)/shard_map/ppermute | solution.py:27
  669.7 3.4 fusion.141
  673.1 3.3 convolution_add_fusion.3
  686.2 4.3 broadcast_multiply_fusion.1
  696.8 3.4 convolution_add_fusion.4
  700.7 5.8 fusion.189
  706.6 6.4 convolution_add_fusion.1
  713.1 5.8 fusion.188
  719.0 6.5 convolution_add_fusion.2
  726.7 5.7 fusion.190
  732.4 6.8 convolution_add_fusion
  740.9 2.9 copy.240
  743.8 8.8 add_convert_fusion.3
  755.9 3.1 copy.249
  760.6 4.6 fusion.130
  765.3 6.6 add_convert_fusion.2
  782.1 37.0 %all-reduce.7 = (f32[1024]{0:T(1024)S(1)}, f32[1024]{0:T(1024)S(1)}) all-reduce(f32[1024]{0:T(1024)S(1)} %add.370, f32[1024]{0:T(1024)S(1)} %add.377), channel_id=4, replica_groups=mesh['batch'=4,'seq'=8] {'batch','seq'}, use_global_device_ids=true, to_apply=%region_30.31.clone | all-reduce | flops 2048 | bytes 16384
  820.3 4.0 fusion.101
  825.8 103.1 %reduce-scatter.10.cloned.1.call-done = f32[32,128]{1,0:T(8,128)} async-done(((f32[1024,128]{1,0:T(8,128)}), f32[32,128]{1,0:T(8,128)}) %reduce-scatter.10.cloned.1.call-update) | async-done | bytes 16400 | tf_op jit(solution)/shard_map/reduce_scatter | solution.py:382
  928.9 143.7 %reduce-scatter.14.cloned.1.call-done = f32[1024,32]{0,1:T(8,128)} async-done(((f32[1024,1024]{0,1:T(8,128)}), f32[1024,32]{0,1:T(8,128)}) %reduce-scatter.14.cloned.1.call-update) | async-done | bytes 131088 | tf_op jit(solution)/shard_map/reduce_scatter | solution.py:384
  1072.6 143.7 %reduce-scatter.8.cloned.1.call-done = f32[32,1024]{1,0:T(8,128)} async-done(((f32[1024,1024]{1,0:T(8,128)}), f32[32,1024]{1,0:T(8,128)}) %reduce-scatter.8.cloned.1.call-update) | async-done | bytes 131088 | tf_op jit(solution)/shard_map/reduce_scatter | solution.py:381
  1216.3 159.3 %reduce-scatter.18.cloned.1.call-done = f32[32,3072]{1,0:T(8,128)} async-done(((f32[1024,3072]{1,0:T(8,128)}), f32[32,3072]{1,0:T(8,128)}) %reduce-scatter.18.cloned.1.call-update) | async-done | bytes 393232 | tf_op jit(solution)/shard_map/reduce_scatter | solution.py:387
  1375.6 162.4 %reduce-scatter.16.cloned.1.call-done = f32[32,3072]{1,0:T(8,128)} async-done(((f32[1024,3072]{1,0:T(8,128)}), f32[32,3072]{1,0:T(8,128)}) %reduce-scatter.16.cloned.1.call-update) | async-done | bytes 393232 | tf_op jit(solution)/shard_map/reduce_scatter | solution.py:386
  1538.0 160.9 %reduce-scatter.20.cloned.1.call-done = f32[3072,32]{0,1:T(8,128)} async-done(((f32[3072,1024]{0,1:T(8,128)}), f32[3072,32]{0,1:T(8,128)}) %reduce-scatter.20.cloned.1.call-update) | async-done | bytes 393232 | tf_op jit(solution)/shard_map/reduce_scatter | solution.py:388
  (541 shorter events, 247.0 us)
Async XLA Ops:
  7.2 68.5 %copy-start.96 = (bf16[32,128]{1,0:T(8,128)(2,1)S(1)}, bf16[32,128]{1,0:T(8,128)(2,1)}, u32[]{:S(2)}) copy-start(bf16[32,128]{1,0:T(8,128)(2,1)} %param.29) | copy-start | bytes 24580
  7.2 136.1 %copy-start.97 = (bf16[32,128]{1,0:T(8,128)(2,1)S(1)}, bf16[32,128]{1,0:T(8,128)(2,1)}, u32[]{:S(2)}) copy-start(bf16[32,128]{1,0:T(8,128)(2,1)} %param.30) | copy-start | bytes 24580
  7.2 237.5 %all-gather.8.cloned.1.call-start = ((), (), s32[]{:S(2)}) async-start(), calls=%async_computation.7 | async-start | bytes 2162688 | tf_op jit(solution)/shard_map/all_gather | solution.py:114
  7.9 266.3 %all-gather.10.cloned.1.call-start = ((), (), s32[]{:S(2)}) async-start(), calls=%async_computation.8 | async-start | bytes 2162688 | tf_op jit(solution)/shard_map/all_gather | solution.py:117
  8.7 274.4 %all-gather.12.cloned.1.call-start = ((), (), s32[]{:S(2)}) async-start(), calls=%async_computation.9 | async-start | bytes 6488064 | tf_op jit(solution)/shard_map/all_gather | solution.py:119
  9.4 200.0 %copy-start.6 = (bf16[4,256,1024]{2,1,0:T(8,128)(2,1)S(1)}, bf16[4,256,1024]{2,1,0:T(8,128)(2,1)}, u32[]{:S(2)}) copy-start(bf16[4,256,1024]{2,1,0:T(8,128)(2,1)} %param.24) | copy-start | bytes 6291460
  9.4 281.6 %all-gather.14.cloned.1.call-start = ((), (), s32[]{:S(2)}) async-start(), calls=%async_computation.10 | async-start | bytes 6488064 | tf_op jit(solution)/shard_map/all_gather | solution.py:120
  10.0 344.2 %all-gather.16.cloned.1.call-start = ((), (), s32[]{:S(2)}) async-start(), calls=%async_computation.11 | async-start | bytes 6488064 | tf_op jit(solution)/shard_map/all_gather | solution.py:121
  73.4 159.8 %copy-start.83 = (f32[1024]{0:T(1024)}, f32[1024]{0:T(1024)S(1)}, u32[]{:S(2)}) copy-start(f32[1024]{0:T(1024)S(1)} %convert_element_type.238) | copy-start | bytes 12292
  75.5 134.0 %copy-start.92 = (f32[1,2,2,128]{3,1,2,0:T(2,128)}, f32[1,2,2,128]{3,1,2,0:T(2,128)S(1)}, u32[]{:S(2)}) copy-start(f32[1,2,2,128]{3,1,2,0:T(2,128)S(1)} %copy.316) | copy-start | bytes 6148
  75.5 134.5 %copy-start.88 = (f32[512]{0:T(512)}, f32[512]{0:T(512)S(1)}, u32[]{:S(2)}) copy-start(f32[512]{0:T(512)S(1)} %rsqrt.50) | copy-start | bytes 6148
  75.5 133.9 %copy-start.94 = (f32[1,2,2,128]{3,1,2,0:T(2,128)}, f32[1,2,2,128]{3,1,2,0:T(2,128)S(1)}, u32[]{:S(2)}) copy-start(f32[1,2,2,128]{3,1,2,0:T(2,128)S(1)} %copy.320) | copy-start | bytes 6148
  75.5 134.5 %copy-start.90 = (f32[512]{0:T(512)}, f32[512]{0:T(512)S(1)}, u32[]{:S(2)}) copy-start(f32[512]{0:T(512)S(1)} %rsqrt.53) | copy-start | bytes 6148
  143.3 66.8 %copy-start.37 = (bf16[1024,128]{1,0:T(8,128)(2,1)}, bf16[1024,128]{1,0:T(8,128)(2,1)S(1)}, u32[]{:S(2)}) copy-start(bf16[1024,128]{1,0:T(8,128)(2,1)S(1)} %all_gather.23) | copy-start | bytes 786436
  209.4 22.6 %copy-start.35 = (bf16[1024,128]{1,0:T(8,128)(2,1)}, bf16[1024,128]{1,0:T(8,128)(2,1)S(1)}, u32[]{:S(2)}) copy-start(bf16[1024,128]{1,0:T(8,128)(2,1)S(1)} %all_gather.26) | copy-start | bytes 786436
  210.0 22.0 %copy-start.16 = (bf16[512,1024]{1,0:T(8,128)(2,1)}, bf16[512,1024]{1,0:T(8,128)(2,1)S(1)}, u32[]{:S(2)}) copy-start(bf16[512,1024]{1,0:T(8,128)(2,1)S(1)} %get-tuple-element.725) | copy-start | bytes 3145732
  216.7 20.5 %collective-permute-start = (bf16[2,256,256]{2,1,0:T(8,128)(2,1)}, bf16[2,256,256]{2,1,0:T(8,128)(2,1)}, u32[]{:S(2)}, u32[]{:S(2)}) collective-permute-start(bf16[2,256,256]{2,1,0:T(8,128)(2,1)} %bitcast.584), channel_id=1, source_target_pairs={{0,4},{1,5},{2,6},{3,7},{8,12},{9,13},{10,14},{11,15},{16,20},{17,... | collective-permute-start | bytes 786440 | tf_op jit(solution)/shard_map/ppermute | solution.py:27
  218.7 20.1 %collective-permute-start.1 = (bf16[2,256,256]{2,1,0:T(8,128)(2,1)}, bf16[2,256,256]{2,1,0:T(8,128)(2,1)}, u32[]{:S(2)}, u32[]{:S(2)}) collective-permute-start(bf16[2,256,256]{2,1,0:T(8,128)(2,1)} %bitcast.585), channel_id=1, source_target_pairs={{0,3},{1,4},{2,5},{3,6},{4,7},{8,11},{9,12},{10,13},{11,14},{12,15... | collective-permute-start | bytes 786440 | tf_op jit(solution)/shard_map/ppermute | solution.py:27
  221.6 19.0 %collective-permute-start.2 = (bf16[2,256,256]{2,1,0:T(8,128)(2,1)}, bf16[2,256,256]{2,1,0:T(8,128)(2,1)}, u32[]{:S(2)}, u32[]{:S(2)}) collective-permute-start(bf16[2,256,256]{2,1,0:T(8,128)(2,1)} %bitcast.586), channel_id=1, source_target_pairs={{0,2},{1,3},{2,4},{3,5},{4,6},{5,7},{8,10},{9,11},{10,12},{11,13},... | collective-permute-start | bytes 786440 | tf_op jit(solution)/shard_map/ppermute | solution.py:27
  223.6 18.6 %collective-permute-start.3 = (bf16[2,256,256]{2,1,0:T(8,128)(2,1)}, bf16[2,256,256]{2,1,0:T(8,128)(2,1)}, u32[]{:S(2)}, u32[]{:S(2)}) collective-permute-start(bf16[2,256,256]{2,1,0:T(8,128)(2,1)} %bitcast.587), channel_id=1, source_target_pairs={{0,1},{1,2},{2,3},{3,4},{4,5},{5,6},{6,7},{8,9},{9,10},{10,11},{11... | collective-permute-start | bytes 786440 | tf_op jit(solution)/shard_map/ppermute | solution.py:27
  227.5 598.4 %reduce-scatter.12.cloned.1.call-start = ((), (), s32[]{:S(2)}) async-start(), calls=%async_computation.14 | async-start | bytes 540672 | tf_op jit(solution)/shard_map/reduce_scatter | solution.py:383
  234.7 44.8 %copy-start.22 = (bf16[2,256,1024]{2,1,0:T(8,128)(2,1)}, bf16[2,256,1024]{2,1,0:T(8,128)(2,1)S(1)}, u32[]{:S(2)}) copy-start(bf16[2,256,1024]{2,1,0:T(8,128)(2,1)S(1)} %get-tuple-element.723) | copy-start | bytes 3145732
  234.7 9.2 copy-start.78
  235.9 144.4 %copy-start.85 = (f32[1024]{0:T(1024)}, f32[1024]{0:T(1024)S(1)}, u32[]{:S(2)}) copy-start(f32[1024]{0:T(1024)S(1)} %convert_element_type.248) | copy-start | bytes 12292
  291.1 63.2 %copy-start.55 = (bf16[2,256,1024]{2,1,0:T(8,128)(2,1)S(1)}, bf16[2,256,1024]{2,1,0:T(8,128)(2,1)}, u32[]{:S(2)}) copy-start(bf16[2,256,1024]{2,1,0:T(8,128)(2,1)} %get-tuple-element.728) | copy-start | bytes 3145732
  387.8 9.8 copy-start.4
  408.8 9.8 copy-start.4
  431.9 11.9 collective-permute-start.10
  433.2 28.4 %collective-permute-start.11 = (bf16[2,256,256]{2,1,0:T(8,128)(2,1)S(1)}, bf16[2,256,256]{2,1,0:T(8,128)(2,1)S(1)}, u32[]{:S(2)}, u32[]{:S(2)}) collective-permute-start(bf16[2,256,256]{2,1,0:T(8,128)(2,1)S(1)} %get-tuple-element.739), channel_id=1, source_target_pairs={{4,0},{5,1},{6,2},{7,3},{12,8},{13,9},{14,10},{15,11},{20,16},{21,... | collective-permute-start | bytes 786440 | tf_op jit(solution)/shard_map/ppermute | solution.py:27
  434.5 27.1 %collective-permute-start.8 = (bf16[2,256,256]{2,1,0:T(8,128)(2,1)S(1)}, bf16[2,256,256]{2,1,0:T(8,128)(2,1)S(1)}, u32[]{:S(2)}, u32[]{:S(2)}) collective-permute-start(bf16[2,256,256]{2,1,0:T(8,128)(2,1)S(1)} %get-tuple-element.738), channel_id=1, source_target_pairs={{1,0},{2,1},{3,2},{4,3},{5,4},{6,5},{7,6},{9,8},{10,9},{11,10},{12... | collective-permute-start | bytes 786440 | tf_op jit(solution)/shard_map/ppermute | solution.py:27
  435.8 25.8 %collective-permute-start.9 = (bf16[2,256,256]{2,1,0:T(8,128)(2,1)S(1)}, bf16[2,256,256]{2,1,0:T(8,128)(2,1)S(1)}, u32[]{:S(2)}, u32[]{:S(2)}) collective-permute-start(bf16[2,256,256]{2,1,0:T(8,128)(2,1)S(1)} %get-tuple-element.741), channel_id=1, source_target_pairs={{2,0},{3,1},{4,2},{5,3},{6,4},{7,5},{10,8},{11,9},{12,10},{13,11},... | collective-permute-start | bytes 786440 | tf_op jit(solution)/shard_map/ppermute | solution.py:27
  438.8 27.4 %copy-start.44 = (f32[1024,128]{0,1:T(8,128)S(1)}, f32[1024,128]{0,1:T(8,128)}, u32[]{:S(2)}) copy-start(f32[1024,128]{0,1:T(8,128)} %copy-done.43) | copy-start | bytes 1572868
  438.8 27.4 %copy-start.46 = (f32[1024,128]{0,1:T(8,128)S(1)}, f32[1024,128]{0,1:T(8,128)}, u32[]{:S(2)}) copy-start(f32[1024,128]{0,1:T(8,128)} %copy-done.45) | copy-start | bytes 1572868
  438.8 27.4 %copy-start.82 = (f32[512,64]{0,1:T(8,128)S(1)}, f32[512,64]{0,1:T(8,128)}, u32[]{:S(2)}) copy-start(f32[512,64]{0,1:T(8,128)} %get-tuple-element.761) | copy-start | bytes 393220
  468.3 23.2 %copy-start.50 = (f32[512,128]{0,1:T(8,128)}, f32[512,128]{0,1:T(8,128)S(1)}, u32[]{:S(2)}) copy-start(f32[512,128]{0,1:T(8,128)S(1)} %get-tuple-element.751) | copy-start | bytes 786436
  469.2 23.7 %collective-permute-start.4 = (bf16[2,256,256]{2,1,0:T(8,128)(2,1)}, bf16[2,256,256]{2,1,0:T(8,128)(2,1)}, u32[]{:S(2)}, u32[]{:S(2)}) collective-permute-start(bf16[2,256,256]{2,1,0:T(8,128)(2,1)} %bitcast.90), channel_id=1, source_target_pairs={{0,4},{1,5},{2,6},{3,7},{8,12},{9,13},{10,14},{11,15},{16,20},{17,... | collective-permute-start | bytes 786440 | tf_op jit(solution)/shard_map/ppermute | solution.py:27
  481.9 12.7 collective-permute-start.5
  483.9 14.1 collective-permute-start.6
  486.9 12.8 collective-permute-start.7
  492.9 10.3 copy-start.87
  524.2 41.6 %copy-start.30 = (f32[512,1024]{1,0:T(8,128)}, f32[512,1024]{1,0:T(8,128)S(1)}, u32[]{:S(2)}) copy-start(f32[512,1024]{1,0:T(8,128)S(1)} %get-tuple-element.775) | copy-start | bytes 6291460
  524.3 9.7 slice-start.3
  524.5 9.5 copy-start.20
  524.5 9.4 slice-start.4
  524.6 14.8 slice-start.1
  573.3 9.8 copy-start.2
  594.4 9.8 copy-start.2
  617.4 46.1 %copy-start.23 = (bf16[2,256,1024]{2,1,0:T(8,128)(2,1)S(1)}, bf16[2,256,1024]{2,1,0:T(8,128)(2,1)}, u32[]{:S(2)}) copy-start(bf16[2,256,1024]{2,1,0:T(8,128)(2,1)} %copy-done.22) | copy-start | bytes 3145732
  617.5 46.5 %copy-start.53 = (bf16[2,256,1024]{2,1,0:T(8,128)(2,1)S(1)}, bf16[2,256,1024]{2,1,0:T(8,128)(2,1)}, u32[]{:S(2)}) copy-start(bf16[2,256,1024]{2,1,0:T(8,128)(2,1)} %get-tuple-element.722) | copy-start | bytes 3145732
  617.5 46.5 %copy-start.62 = (f32[2,256,256]{2,1,0:T(8,128)S(1)}, f32[2,256,256]{2,1,0:T(8,128)}, u32[]{:S(2)}) copy-start(f32[2,256,256]{2,1,0:T(8,128)} %copy-done.61) | copy-start | bytes 1572868
  617.6 8.8 collective-permute-start.12
  619.0 18.2 %collective-permute-start.13 = (bf16[2,256,256]{2,1,0:T(8,128)(2,1)S(1)}, bf16[2,256,256]{2,1,0:T(8,128)(2,1)S(1)}, u32[]{:S(2)}, u32[]{:S(2)}) collective-permute-start(bf16[2,256,256]{2,1,0:T(8,128)(2,1)S(1)} %get-tuple-element.745), channel_id=1, source_target_pairs={{2,0},{3,1},{4,2},{5,3},{6,4},{7,5},{10,8},{11,9},{12,10},{13,11},... | collective-permute-start | bytes 786440 | tf_op jit(solution)/shard_map/ppermute | solution.py:27
  620.3 20.0 %collective-permute-start.14 = (bf16[2,256,256]{2,1,0:T(8,128)(2,1)S(1)}, bf16[2,256,256]{2,1,0:T(8,128)(2,1)S(1)}, u32[]{:S(2)}, u32[]{:S(2)}) collective-permute-start(bf16[2,256,256]{2,1,0:T(8,128)(2,1)S(1)} %get-tuple-element.744), channel_id=1, source_target_pairs={{3,0},{4,1},{5,2},{6,3},{7,4},{11,8},{12,9},{13,10},{14,11},{15,12... | collective-permute-start | bytes 786440 | tf_op jit(solution)/shard_map/ppermute | solution.py:27
  621.6 39.9 %collective-permute-start.15 = (bf16[2,256,256]{2,1,0:T(8,128)(2,1)S(1)}, bf16[2,256,256]{2,1,0:T(8,128)(2,1)S(1)}, u32[]{:S(2)}, u32[]{:S(2)}) collective-permute-start(bf16[2,256,256]{2,1,0:T(8,128)(2,1)S(1)} %get-tuple-element.743), channel_id=1, source_target_pairs={{4,0},{5,1},{6,2},{7,3},{12,8},{13,9},{14,10},{15,11},{20,16},{21,... | collective-permute-start | bytes 786440 | tf_op jit(solution)/shard_map/ppermute | solution.py:27
  665.4 263.5 %reduce-scatter.10.cloned.1.call-start = ((), (), s32[]{:S(2)}) async-start(), calls=%async_computation.13 | async-start | bytes 540672 | tf_op jit(solution)/shard_map/reduce_scatter | solution.py:382
  669.6 403.0 %reduce-scatter.14.cloned.1.call-start = ((), (), s32[]{:S(2)}) async-start(), calls=%async_computation.15 | async-start | bytes 4325376 | tf_op jit(solution)/shard_map/reduce_scatter | solution.py:384
  676.5 539.9 %reduce-scatter.8.cloned.1.call-start = ((), (), s32[]{:S(2)}) async-start(), calls=%async_computation.12 | async-start | bytes 4325376 | tf_op jit(solution)/shard_map/reduce_scatter | solution.py:381
  700.2 675.4 %reduce-scatter.18.cloned.1.call-start = ((), (), s32[]{:S(2)}) async-start(), calls=%async_computation.17 | async-start | bytes 12976128 | tf_op jit(solution)/shard_map/reduce_scatter | solution.py:387
  713.0 825.0 %reduce-scatter.16.cloned.1.call-start = ((), (), s32[]{:S(2)}) async-start(), calls=%async_computation.16 | async-start | bytes 12976128 | tf_op jit(solution)/shard_map/reduce_scatter | solution.py:386
  725.5 973.5 %reduce-scatter.20.cloned.1.call-start = ((), (), s32[]{:S(2)}) async-start(), calls=%async_computation.18 | async-start | bytes 12976128 | tf_op jit(solution)/shard_map/reduce_scatter | solution.py:388
  743.8 10.5 copy-start.51
  765.3 8.1 copy-start.27
  779.4 40.8 %copy-start.95 = (f32[1,2,2,128]{3,1,2,0:T(2,128)S(1)}, f32[1,2,2,128]{3,1,2,0:T(2,128)}, u32[]{:S(2)}) copy-start(f32[1,2,2,128]{3,1,2,0:T(2,128)} %copy-done.94) | copy-start | bytes 6148
  779.4 40.9 %copy-start.93 = (f32[1,2,2,128]{3,1,2,0:T(2,128)S(1)}, f32[1,2,2,128]{3,1,2,0:T(2,128)}, u32[]{:S(2)}) copy-start(f32[1,2,2,128]{3,1,2,0:T(2,128)} %copy-done.92) | copy-start | bytes 6148
  (80 other events, 250.1 us)
Sparse Core Ops, SparseCore 0:
  11.0 59.3 all-gather.7
  73.4 55.6 all-gather.9
  132.0 69.8 all-gather.11
  204.6 78.8 all-gather.13
  286.2 68.0 all-gather.15
  665.5 130.2 reduce-scatter.11
  798.8 130.0 reduce-scatter.9
  931.8 140.8 reduce-scatter.13
  1075.5 140.8 reduce-scatter.7
  1222.8 152.7 reduce-scatter.17
  1383.3 154.7 reduce-scatter.15
  1544.5 154.4 reduce-scatter.19
where the time goes:
time: 1710 us
  waiting for transfers between devices  993 us (58%)
  matrix products  247 us (14%)
  blocking collectives  223 us (13%)
  local copies, waits for them, and re-layouts  116 us (7%)
  other arithmetic  66.2 us (4%)
  starting transfers between devices  42.7 us (2%)
  between operations  17.3 us (1%)
    reduce_scatter x1, waiting for transfers between devices, on_device(): lax.psum_scatter(sums[6], ('batch', 'seq'), scatter_dimension=0, tiled=True)  162 us
    reduce_scatter x1, waiting for transfers between devices, on_device(): lax.psum_scatter(sums[8], ('batch', 'seq'), scatter_dimension=1, tiled=True)  161 us
    reduce_scatter x1, waiting for transfers between devices, on_device(): lax.psum_scatter(sums[7], ('batch', 'seq'), scatter_dimension=0, tiled=True)  159 us
    reduce_scatter x1, waiting for transfers between devices, on_device(): lax.psum_scatter(sums[1], ('batch', 'seq'), scatter_dimension=0, tiled=True)  144 us
    reduce_scatter x1, waiting for transfers between devices, on_device(): lax.psum_scatter(sums[4], ('batch', 'seq'), scatter_dimension=1, tiled=True)  144 us
    reduce_scatter x1, waiting for transfers between devices, on_device(): lax.psum_scatter(sums[2], ('batch', 'seq'), scatter_dimension=0, tiled=True)  103 us
    unnamed x3, blocking collectives  89.5 us
    all_gather x1, blocking collectives, fetch_weights(): lax.all_gather(key_weight, ('batch', 'seq'), axis=0, tiled=True)  67.6 us
  transfers between devices with their start and end apart: 28, of which 14 were waited for; matrix products, arithmetic and copies ran while one was open for 12% of the time, Pallas kernels for 0%

commit v1 on v0

v1 whole, which is shorter than its diff:
```python
import functools

import jax
import jax.numpy as jnp
from jax import lax
from jax.experimental import pallas as pl
from jax.experimental.pallas import tpu as pltpu
from jax.sharding import PartitionSpec as P

WINDOW = 1024
FF_CHUNKS = 6
MESH_ID = pl.DeviceIdType.MESH
MIB = 1 << 20


def rotate(values, cosine, sine):
    half_width = values.shape[-1] // 2
    turned = jnp.concatenate([-values[..., half_width:], values[..., :half_width]], axis=-1)
    return values * cosine + turned * sine


def tables(positions, head_dim):
    inverse = 10000.0 ** (-2.0 * jnp.arange(head_dim // 2, dtype=jnp.float32) / head_dim)
    angle = positions.astype(jnp.float32)[:, None] * inverse[None, :]
    cosine, sine = jnp.cos(angle), jnp.sin(angle)
    return (
        jnp.concatenate([cosine, cosine], axis=-1),
        jnp.concatenate([sine, sine], axis=-1),
    )


def rms_scale(values, gain):
    return values * lax.rsqrt(jnp.mean(values * values, axis=-1, keepdims=True) + 1e-06) * gain


def gated(gate, up_part):
    return jax.nn.gelu(gate, approximate=True) * up_part


def matmul(left, right):
    return jnp.dot(left, right, preferred_element_type=jnp.float32)


def left_times(left, right):
    return lax.dot_general(
        left, right, (((0,), (0,)), ((), ())), preferred_element_type=jnp.float32
    )


def right_times(left, right):
    return lax.dot_general(
        left, right, (((1,), (1,)), ((), ())), preferred_element_type=jnp.float32
    )


def place():
    batch, seq = lax.axis_index("batch"), lax.axis_index("seq")
    return batch // 2, lax.rem(batch, 2), seq // 2, lax.rem(seq, 2)


def device(x, c, z, y):
    return (x * 2 + c, z * 2 + y)


def greet(partners):
    barrier = pltpu.get_barrier_semaphore()
    for partner in partners:
        pl.semaphore_signal(barrier, inc=1, device_id=partner, device_id_type=MESH_ID)
    pl.semaphore_wait(barrier, len(partners))


def neighbours():
    x, c, z, y = place()
    return [
        device(x, c, lax.rem(z + 1, 4), y),
        device(x, c, lax.rem(z + 2, 4), y),
        device(x, c, lax.rem(z + 3, 4), y),
        device(1 - x, c, z, y),
        device(x, c, z, 1 - y),
        device(x, 1 - c, z, y),
    ]


def send(source, target, send_sem, recv_sem, partner):
    copy = pltpu.make_async_remote_copy(
        src_ref=source,
        dst_ref=target,
        send_sem=send_sem,
        recv_sem=recv_sem,
        device_id=partner,
        device_id_type=MESH_ID,
    )
    copy.start()
    return copy


class Gather:
    STEPS = 4
    SEMS = 8

    def __init__(self, shard, full, sems, local_sem, chunks):
        self.shard, self.full, self.sems, self.local_sem = shard, full, sems, local_sem
        self.chunks = chunks
        self.copies = {}

    def go(self, chunk, slot, source, partner):
        self.copies[chunk, slot] = send(
            source, source, self.sems.at[0, chunk, slot], self.sems.at[1, chunk, slot], partner
        )

    def arrived(self, chunk, slot):
        self.copies[chunk, slot].wait_recv()

    def step(self, number, chunk):
        x, c, z, y = place()
        start, middle, end = self.chunks[chunk]
        full = self.full
        whole = pl.ds(start, end - start)
        first, second = pl.ds(start, middle - start), pl.ds(middle, end - middle)
        if number == 0:
            mine = full.at[x, c, z, y, :, whole]
            keep = pltpu.make_async_copy(
                self.shard.at[:, whole], mine, self.local_sem.at[chunk]
            )
            keep.start()
            self.copies[chunk, "keep"] = keep
            for hop in (1, 2, 3):
                self.copies[chunk, hop - 1] = send(
                    self.shard.at[:, whole],
                    mine,
                    self.sems.at[0, chunk, hop - 1],
                    self.sems.at[1, chunk, hop - 1],
                    device(x, c, lax.rem(z + hop, 4), y),
                )
        elif number == 1:
            self.copies[chunk, "keep"].wait()
            for slot in (0, 1, 2):
                self.arrived(chunk, slot)
            self.go(chunk, 3, full.at[x, c, :, y, :, first], device(x, c, z, 1 - y))
            self.go(chunk, 4, full.at[x, c, :, y, :, second], device(1 - x, c, z, y))
        elif number == 2:
            self.arrived(chunk, 3)
            self.go(chunk, 5, full.at[x, c, :, :, :, first], device(1 - x, c, z, y))
            self.arrived(chunk, 4)
            self.go(chunk, 6, full.at[:, c, :, y, :, second], device(x, c, z, 1 - y))
        elif number == 3:
            self.arrived(chunk, 5)
            self.arrived(chunk, 6)
            self.go(chunk, 7, full.at[:, c, :, :, :, whole], device(x, 1 - c, z, y))
        else:
            self.arrived(chunk, 7)

    def drain(self):
        for (_, slot), copy in self.copies.items():
            if slot != "keep":
                copy.wait_send()


def gather_kernel(chunks, shard_ref, full_ref, sems, local_sem):
    greet(neighbours())
    gather = Gather(shard_ref, full_ref, sems, local_sem, chunks)
    for tick in range(len(chunks) + Gather.STEPS):
        for number in range(Gather.STEPS + 1):
            chunk = tick - number
            if 0 <= chunk < len(chunks):
                gather.step(number, chunk)
    gather.drain()


def gather_all(shard, chunks):
    rows, columns = shard.shape
    count = len(chunks)
    full = pl.pallas_call(
        functools.partial(gather_kernel, chunks),
        out_shape=jax.ShapeDtypeStruct((2, 2, 4, 2, rows, columns), shard.dtype),
        in_specs=[pl.BlockSpec(memory_space=pl.ANY)],
        out_specs=pl.BlockSpec(memory_space=pl.ANY),
        scratch_shapes=[
            pltpu.SemaphoreType.DMA((2, count, Gather.SEMS)),
            pltpu.SemaphoreType.DMA((count,)),
        ],
        compiler_params=pltpu.CompilerParams(collective_id=0, has_side_effects=True),
        name="gather_weights",
    )(shard)
    return full.reshape(32 * rows, columns)


class Scatter:
    STEPS = 4
    SEMS = 8

    def __init__(self, own, first, second_a, second_b, third_a, third_b, last, sems):
        self.own = own
        self.first = first
        self.second_a, self.second_b = second_a, second_b
        self.third_a, self.third_b = third_a, third_b
        self.last = last
        self.sems = sems
        self.copies = {}


def add_rows(target, other):
    target[...] = (target[...].astype(jnp.float32) + other[...].astype(jnp.float32)).astype(
        target.dtype
    )


def scatter_kernel(chunks, own_ref, out_ref, *scratch):
    greet(neighbours())
    x, c, z, y = place()
    count = len(chunks)
    sems, local_sems, out_sem = scratch[:3]
    buffers = scratch[3:]
    copies = {}

    def go(chunk, slot, source, target, partner):
        copies[chunk, slot] = send(
            source, target, sems.at[0, chunk, slot], sems.at[1, chunk, slot], partner
        )

    for tick in range(count + 5):
        for number in range(6):
            chunk = tick - number
            if not 0 <= chunk < count:
                continue
            start, middle, end = chunks[chunk]
            width, half = end - start, middle - start
            one, two_a, two_b, three_a, three_b, last, mine, result = buffers[
                8 * chunk : 8 * chunk + 8
            ]
            whole = pl.ds(start, width)
            if number == 0:
                go(chunk, 0, own_ref.at[:, 1 - c, :, :, :, whole], one, device(x, 1 - c, z, y))
                keep = pltpu.make_async_copy(
                    own_ref.at[:, c, :, :, :, whole], mine, local_sems.at[chunk]
                )
                keep.start()
                copies[chunk, "keep"] = keep
            elif number == 1:
                copies[chunk, "keep"].wait()
                copies[chunk, 0].wait_recv()
                for i in range(2):
                    for j in range(4):

                        @pl.loop(0, 2)
                        def _(k):
                            add_rows(one.at[i, j, k], mine.at[i, j, k])

                go(chunk, 1, one.at[1 - x, :, :, :, :half], two_a, device(1 - x, c, z, y))
                go(chunk, 2, one.at[:, :, 1 - y, :, half:], two_b, device(x, c, z, 1 - y))
            elif number == 2:
                copies[chunk, 1].wait_recv()
                for j in range(4):

                    @pl.loop(0, 2)
                    def _(k):
                        add_rows(two_a.at[j, k], one.at[x, j, k, :, :half])

                go(chunk, 3, two_a.at[:, 1 - y], three_a, device(x, c, z, 1 - y))
                copies[chunk, 2].wait_recv()
                for j in range(2):

                    @pl.loop(0, 4)
                    def _(k):
                        add_rows(two_b.at[j, k], one.at[j, k, y, :, half:])

                go(chunk, 4, two_b.at[1 - x], three_b, device(1 - x, c, z, y))
            elif number == 3:
                copies[chunk, 3].wait_recv()

                @pl.loop(0, 4)
                def _(k):
                    mine[0, k, 0, :, :half] = (
                        three_a[k].astype(jnp.float32) + two_a[k, y].astype(jnp.float32)
                    ).astype(mine.dtype)

                copies[chunk, 4].wait_recv()

                @pl.loop(0, 4)
                def _(k):
                    mine[0, k, 0, :, half:] = (
                        three_b[k].astype(jnp.float32) + two_b[x, k].astype(jnp.float32)
                    ).astype(mine.dtype)

                for hop in (1, 2, 3):
                    go(
                        chunk,
                        4 + hop,
                        mine.at[0, lax.rem(z + hop, 4), 0],
                        last.at[hop - 1],
                        device(x, c, lax.rem(z + hop, 4), y),
                    )
            elif number == 4:
                total = mine[0, z, 0].astype(jnp.float32)
                for hop in (1, 2, 3):
                    copies[chunk, 4 + hop].wait_recv()
                    total += last[hop - 1].astype(jnp.float32)
                result[...] = total
                done = pltpu.make_async_copy(result, out_ref.at[:, whole], out_sem.at[chunk])
                done.start()
                copies[chunk, "done"] = done
            else:
                for slot in range(8):
                    copies[chunk, slot].wait_send()
                copies[chunk, "done"].wait()


def scatter_all(own, rows, chunks):
    columns = own.shape[1]
    count = len(chunks)
    scratch = [
        pltpu.SemaphoreType.DMA((2, count, Scatter.SEMS)),
        pltpu.SemaphoreType.DMA((count,)),
        pltpu.SemaphoreType.DMA((count,)),
    ]
    for start, middle, end in chunks:
        n, h = end - start, middle - start
        scratch += [
            pltpu.VMEM((2, 4, 2, rows, n), own.dtype),
            pltpu.VMEM((4, 2, rows, h), own.dtype),
            pltpu.VMEM((2, 4, rows, n - h), own.dtype),
            pltpu.VMEM((4, rows, h), own.dtype),
            pltpu.VMEM((4, rows, n - h), own.dtype),
            pltpu.VMEM((3, rows, n), own.dtype),
            pltpu.VMEM((2, 4, 2, rows, n), own.dtype),
            pltpu.VMEM((rows, n), jnp.float32),
        ]
    return pl.pallas_call(
        functools.partial(scatter_kernel, chunks),
        out_shape=jax.ShapeDtypeStruct((rows, columns), jnp.float32),
        in_specs=[pl.BlockSpec(memory_space=pl.ANY)],
        out_specs=pl.BlockSpec(memory_space=pl.ANY),
        scratch_shapes=scratch,
        compiler_params=pltpu.CompilerParams(
            collective_id=1, has_side_effects=True, vmem_limit_bytes=56 * MIB
        ),
        name="scatter_grads",
    )(own.reshape(2, 2, 4, 2, rows, columns))


def columns_of(width, head_dim, heads, hidden):
    attention = width + 2 * head_dim + 128
    chunks = [(0, 640, attention), (attention, attention + width // 2, attention + width)]
    start = attention + width
    step = 3 * hidden // FF_CHUNKS
    for _ in range(FF_CHUNKS):
        chunks.append((start, start + step // 2, start + step))
        start += step
    return chunks


def stack_ff(gate, up_part, down_t):
    rows, hidden = gate.shape
    parts = [p.reshape(rows, FF_CHUNKS, hidden // FF_CHUNKS) for p in (gate, up_part, down_t)]
    return jnp.stack(parts, axis=2).reshape(rows, 3 * hidden)


def unstack_ff(stacked):
    rows, hidden = stacked.shape[0], stacked.shape[1] // 3
    parts = stacked.reshape(rows, FF_CHUNKS, 3, hidden // FF_CHUNKS)
    return [parts[:, :, i].reshape(rows, hidden) for i in range(3)]


def allowed_pairs(query_place, key_place, starts):
    later = key_place[None, :] <= query_place[:, None]
    inside = query_place[:, None] - key_place[None, :] < WINDOW
    same_doc = key_place[None, :] >= starts[:, None]
    return later & inside & same_doc


def attend_one(query, pairs, starts, query_place, key_place, scale, head_dim):
    keys = pairs[:, :head_dim]
    values = pairs[:, head_dim:]
    allowed = allowed_pairs(query_place, key_place, starts)
    score = jnp.einsum("qhd,kd->hqk", query, keys, preferred_element_type=jnp.float32) * scale
    score = jnp.where(allowed[None], score, -1e30)
    peak = jnp.max(score, axis=-1, keepdims=True)
    log_total = peak + jnp.log(jnp.sum(jnp.exp(score - peak), axis=-1, keepdims=True))
    weights_low = jnp.exp(score - log_total).astype(jnp.bfloat16)
    result = jnp.einsum("hqk,kd->qhd", weights_low, values, preferred_element_type=jnp.float32)
    return (result, log_total[..., 0])


def attend_back(query, pairs, starts, log_total, grad_out, query_place, key_place, scale, head_dim):
    keys = pairs[:, :head_dim]
    values = pairs[:, head_dim:]
    allowed = allowed_pairs(query_place, key_place, starts)
    score = jnp.einsum("qhd,kd->hqk", query, keys, preferred_element_type=jnp.float32) * scale
    score = jnp.where(allowed[None], score, -1e30)
    weights = jnp.exp(score - log_total[..., None])
    weights_low = weights.astype(jnp.bfloat16)
    grad_weights = jnp.einsum("qhd,kd->hqk", grad_out, values, preferred_element_type=jnp.float32)
    grad_values = jnp.einsum(
        "hqk,qhd->kd", weights_low, grad_out, preferred_element_type=jnp.float32
    )
    grad_score = (
        weights * (grad_weights - jnp.sum(weights * grad_weights, axis=-1, keepdims=True))
    ).astype(jnp.bfloat16)
    grad_query = (
        jnp.einsum("hqk,kd->qhd", grad_score, keys, preferred_element_type=jnp.float32) * scale
    )
    grad_keys = (
        jnp.einsum("hqk,qhd->kd", grad_score, query, preferred_element_type=jnp.float32) * scale
    )
    return (grad_query, jnp.concatenate([grad_keys, grad_values], axis=-1))


def shifted(value, axis, steps):
    count = lax.axis_size(axis)
    initial, last = (max(0, -steps), min(count, count - steps))
    return lax.ppermute(value, axis, [(source, source + steps) for source in range(initial, last)])


def on_device(
    own_links,
    tokens,
    segments,
    cotangent,
    first_gain,
    query_weight,
    key_weight,
    value_weight,
    out_weight,
    second_gain,
    gate_weight,
    up_weight,
    down_weight,
):
    seqs, block_len, width = tokens.shape
    head_dim = key_weight.shape[1]
    heads = query_weight.shape[1] // head_dim
    hidden_width = gate_weight.shape[1]
    shard_rows = first_gain.shape[0]
    reach = (WINDOW - 1 + block_len - 1) // block_len
    span = (reach + 1) * block_len
    scale = head_dim ** (-0.5)
    rows = seqs * block_len
    chunks = columns_of(width, head_dim, heads, hidden_width)

    gains = jnp.zeros((shard_rows, 128), first_gain.dtype)
    gains = gains.at[:, 0].set(first_gain).at[:, 1].set(second_gain)
    shard = jnp.concatenate(
        [
            query_weight,
            key_weight,
            value_weight,
            gains,
            out_weight.T,
            stack_ff(gate_weight, up_weight, down_weight.T),
        ],
        axis=1,
    )
    if own_links:
        full = gather_all(shard, chunks)
    else:
        full = lax.all_gather(shard, ("batch", "seq"), axis=0, tiled=True)
    all_segments = lax.all_gather(segments, "seq", axis=1, tiled=True)
    query_full = full[:, :width]
    key_full = full[:, width : width + head_dim]
    value_full = full[:, width + head_dim : width + 2 * head_dim]
    gains_full = full[:, width + 2 * head_dim : chunks[0][2]].astype(jnp.float32)
    gain_one, gain_two = gains_full[:, 0], gains_full[:, 1]
    out_t = full[:, chunks[1][0] : chunks[1][2]]
    gate_full, up_full, down_t = unstack_ff(full[:, chunks[2][0] :])

    starts = jnp.sum(all_segments[:, None, :] < segments[:, :, None], axis=-1, dtype=jnp.int32)
    query_place = jnp.arange(block_len, dtype=jnp.int32) + lax.axis_index("seq") * block_len
    key_place = query_place[0] - reach * block_len + jnp.arange(span, dtype=jnp.int32)
    cosine, sine = tables((query_place[None, :] - starts).reshape(-1), head_dim)

    def forward_item(item):
        return attend_one(item[0], item[1], item[2], query_place, key_place, scale, head_dim)

    def backward_item(item):
        return attend_back(
            item[0], item[1], item[2], item[3], item[4], query_place, key_place, scale, head_dim
        )

    inputs = tokens.reshape(rows, width).astype(jnp.float32)
    normed_one = rms_scale(inputs, gain_one).astype(jnp.bfloat16)
    query = rotate(
        matmul(normed_one, query_full).reshape(rows, heads, head_dim),
        cosine[:, None, :],
        sine[:, None, :],
    ).astype(jnp.bfloat16)
    key_rot = rotate(matmul(normed_one, key_full), cosine, sine).astype(jnp.bfloat16)
    value_low = matmul(normed_one, value_full).astype(jnp.bfloat16)
    own_pairs = jnp.concatenate([key_rot, value_low], axis=-1).reshape(
        seqs, block_len, 2 * head_dim
    )
    pieces = [shifted(own_pairs, "seq", distance) for distance in range(reach, 0, -1)]
    window_pairs = jnp.concatenate(pieces + [own_pairs], axis=1)
    query_seq = query.reshape(seqs, block_len, heads, head_dim)
    attended, log_total = lax.map(forward_item, (query_seq, window_pairs, starts))
    attended_low = attended.reshape(rows, heads * head_dim).astype(jnp.bfloat16)
    mixed = inputs + right_times(attended_low, out_t)
    normed_two = rms_scale(mixed, gain_two).astype(jnp.bfloat16)
    gate = matmul(normed_two, gate_full)
    up_part = matmul(normed_two, up_full)
    hidden = gated(gate, up_part).astype(jnp.bfloat16)
    output = (mixed + right_times(hidden, down_t)).astype(jnp.bfloat16)

    grad_rows = cotangent.reshape(rows, width)
    grad_down_t = left_times(grad_rows, hidden)
    grad_hidden = matmul(grad_rows, down_t)
    _, pull_gated = jax.vjp(gated, gate, up_part)
    grad_gate, grad_up = pull_gated(grad_hidden)
    grad_gate = grad_gate.astype(jnp.bfloat16)
    grad_up = grad_up.astype(jnp.bfloat16)
    grad_gate_w = left_times(normed_two, grad_gate)
    grad_up_w = left_times(normed_two, grad_up)
    grad_normed_two = right_times(grad_gate, gate_full) + right_times(grad_up, up_full)
    _, pull_second = jax.vjp(rms_scale, mixed, gain_two)
    grad_mixed, grad_gain_two = pull_second(grad_normed_two)
    grad_mixed = grad_mixed + grad_rows.astype(jnp.float32)
    grad_branch = grad_mixed.astype(jnp.bfloat16)
    grad_out_t = left_times(grad_branch, attended_low)
    grad_attended = matmul(grad_branch, out_t).astype(jnp.bfloat16)
    grad_query, grad_pairs = lax.map(
        backward_item,
        (
            query_seq,
            window_pairs,
            starts,
            log_total,
            grad_attended.reshape(seqs, block_len, heads, head_dim),
        ),
    )
    own_grad = grad_pairs[:, reach * block_len :]
    for distance in range(1, reach + 1):
        piece = grad_pairs[:, (reach - distance) * block_len : (reach - distance + 1) * block_len]
        own_grad = own_grad + shifted(piece.astype(jnp.bfloat16), "seq", -distance).astype(
            piece.dtype
        )
    grad_key_rot = own_grad[..., :head_dim].reshape(rows, head_dim)
    grad_value = own_grad[..., head_dim:].reshape(rows, head_dim).astype(jnp.bfloat16)
    grad_q = rotate(
        grad_query.reshape(rows, heads, head_dim), cosine[:, None, :], -sine[:, None, :]
    )
    grad_q = grad_q.reshape(rows, heads * head_dim).astype(jnp.bfloat16)
    grad_k = rotate(grad_key_rot, cosine, -sine).astype(jnp.bfloat16)
    grad_qkv = jnp.concatenate([grad_q, grad_k, grad_value], axis=1)
    grad_qkv_w = left_times(normed_one, grad_qkv)
    grad_normed_one = right_times(grad_qkv, full[:, : width + 2 * head_dim])
    _, pull_first = jax.vjp(rms_scale, inputs, gain_one)
    grad_x, grad_gain_one = pull_first(grad_normed_one)
    grad_input = (grad_x + grad_mixed).astype(jnp.bfloat16)

    grad_gains = jnp.zeros((width, 128), jnp.float32)
    grad_gains = grad_gains.at[:, 0].set(grad_gain_one).at[:, 1].set(grad_gain_two)
    grads = jnp.concatenate(
        [
            grad_qkv_w,
            grad_gains,
            grad_out_t,
            stack_ff(grad_gate_w, grad_up_w, grad_down_t),
        ],
        axis=1,
    ).astype(jnp.bfloat16)
    if own_links:
        share = scatter_all(grads, shard_rows, chunks)
    else:
        share = lax.psum_scatter(grads, ("batch", "seq"), scatter_dimension=0, tiled=True)
        share = share.astype(jnp.float32)
    share_gate, share_up, share_down_t = unstack_ff(share[:, chunks[2][0] :])
    return (
        output.reshape(tokens.shape),
        grad_input.reshape(tokens.shape),
        share[:, width + 2 * head_dim],
        share[:, :width],
        share[:, width : width + head_dim],
        share[:, width + head_dim : width + 2 * head_dim],
        share[:, chunks[1][0] : chunks[1][2]].T,
        share[:, width + 2 * head_dim + 1],
        share_gate,
        share_up,
        share_down_t.T,
    )


def solution(mesh):
    both = ("batch", "seq")
    rows_split, columns_split = P(both, None), P(None, both)
    tokens_split, gain_split = P("batch", "seq", None), P(both)
    weights = (
        gain_split,
        rows_split,
        rows_split,
        rows_split,
        columns_split,
        gain_split,
        rows_split,
        rows_split,
        columns_split,
    )
    in_specs = (tokens_split, P("batch", "seq"), tokens_split) + weights
    out_specs = (tokens_split, tokens_split) + weights
    own_links = (mesh.shape["batch"], mesh.shape["seq"]) == (4, 8)
    return jax.shard_map(
        functools.partial(on_device, own_links),
        mesh=mesh,
        in_specs=in_specs,
        out_specs=out_specs,
        check_vma=False,
    )
```

time: 1710 us -> 907 us (0.53)
  waiting for transfers between devices: 993 us -> 0.02 us
  Pallas kernels: 0 us -> 240 us
  blocking collectives: 223 us -> 32 us
  local copies, waits for them, and re-layouts: 116 us -> 279 us
  other arithmetic: 66.2 us -> 95.1 us
  matrix products: 247 us -> 222 us
  starting transfers between devices: 42.7 us -> 20.1 us
    reduce_scatter x7 -> x0, waiting for transfers between devices: 873 us -> none  [the longest x1 162 us: on_device(): lax.psum_scatter(sums[6], ('batch', 'seq'), scatter_dimension=0, tiled=True)]
    pallas_call x0 -> x2, Pallas kernels: none -> 240 us  [the longest x1 122 us: scatter_all(): pl.pallas_call(functools.partial(scatter_kernel, chunks), out_shape=jax.S...]
    all_gather x2 -> x1, blocking collectives: 134 us -> 32 us  [on_device(): all_segments = lax.all_gather(segments, 'seq', axis=1, tiled=True)]
    unnamed x3 -> x0, blocking collectives: 89.5 us -> none
    ppermute x16 -> x8, waiting for transfers between devices: 63.3 us -> 0.02 us  [shifted(): lax.ppermute(value, axis, [(source, source + steps) for source in range(i...]
    another operation x13 -> x10, local copies, waits for them, and re-layouts: 6.79 us -> 62.4 us  [the longest x5 44.7 us: stack_ff(): return jnp.stack(parts, axis=2).reshape(rows, 3 * hidden)]
    all_gather x5 -> x0, waiting for transfers between devices: 53.7 us -> none  [the longest x1 53.7 us: fetch_weights(): lax.all_gather(down_weight, ('batch', 'seq'), axis=1, tiled=True)]
    concatenate x0 -> x2, local copies, waits for them, and re-layouts: none -> 50.8 us  [the longest x1 50.7 us: on_device(): jnp.concatenate([grad_qkv_w, grad_gains, grad_out_t, stack_ff(grad_gate_w...]
  transfers between devices with their start and end apart: 28 -> 8, of which waited for: 14 -> 0; matrix products, arithmetic and copies ran while one was open for 12% -> 25% of each run, Pallas kernels for 0% -> 0%
where the time goes in v1:
time: 907 us; the launch traced here: 892 us
  local copies, waits for them, and re-layouts  279 us (31%)
  Pallas kernels  240 us (26%)
  matrix products  222 us (24%)
  other arithmetic  95.1 us (10%)
  blocking collectives  32 us (4%)
  starting transfers between devices  20.1 us (2%)
    pallas_call x1, Pallas kernels, scatter_all(): pl.pallas_call(functools.partial(scatter_kernel, chunks), out_shape=jax.S...  122 us
    pallas_call x1, Pallas kernels, gather_all(): pl.pallas_call(functools.partial(gather_kernel, chunks), out_shape=jax.Sh...  118 us
    dot_general x7, matrix products, matmul(): return jnp.dot(left, right, preferred_element_type=jnp.float32)  54.1 us
    concatenate x1, local copies, waits for them, and re-layouts, on_device(): jnp.concatenate([grad_qkv_w, grad_gains, grad_out_t, stack_ff(grad_gate_w...  50.7 us
    dot_general x5, matrix products, right_times(): lax.dot_general(left, right, (((1,), (1,)), ((), ())), preferred_element_...  44.9 us
    another operation x5, local copies, waits for them, and re-layouts, stack_ff(): return jnp.stack(parts, axis=2).reshape(rows, 3 * hidden)  44.7 us
    unnamed x111, local copies, waits for them, and re-layouts  40.7 us
    dot_general x5, matrix products, left_times(): lax.dot_general(left, right, (((0,), (0,)), ((), ())), preferred_element_...  40.4 us
  transfers between devices with their start and end apart: 8, of which 0 were waited for; matrix products, arithmetic and copies ran while one was open for 25% of the time, Pallas kernels for 0%

profile of v1, /device:TPU:0, one launch (start us, length us, event | category | flops | bytes accessed | tf_op | source)
XLA Modules:
  0.0 892.3 jit_solution(11682989315045386781)
XLA Ops:
  11.9 118.2 %gather_weights.1 = bf16[2,2,4,2,32,11648]{5,4,3,2,1,0:T(8,128)(2,1)} custom-call(bf16[32,11648]{1,0:T(8,128)(2,1)} %copy-done.32), custom_call_target="tpu_custom_call" | custom-call | tf_op jit(solution)/shard_map/gather_weights/pallas_call | solution.py:173
  136.2 32.0 %all_gather.3 = s32[4,2048]{1,0:T(4,128)S(1)} all-gather(s32[4,256]{1,0:T(4,128)S(1)} %copy-done.41), channel_id=1, replica_groups=mesh['batch'=4,'seq'=8] {'seq'}, dimensions={1}, use_global_device_ids=true | all-gather | bytes 36864 | tf_op jit(solution)/shard_map/all_gather | solution.py:457
  175.6 7.4 collective-permute-start.1
  185.2 3.3 collective-permute-start.3
  188.5 3.1 slice_bitcast_fusion.9
  191.5 16.7 %slice.246 = bf16[1024,9216]{1,0:T(8,128)(2,1)} slice(bf16[1024,11648]{1,0:T(8,128)(2,1)} %bitcast.304), slice={[0:1024], [2432:11648]} | slice | bytes 37748736 | tf_op jit(solution)/shard_map/slice | solution.py:464
  210.1 2.9 copy.111
  213.0 24.6 %copy.149 = bf16[1024,9216]{0,1:T(8,128)(2,1)} copy(bf16[1024,9216]{1,0:T(8,128)(2,1)} %slice.246) | data formatting | bytes 37748736
  237.6 14.0 %fusion.97 = (bf16[1024,6,1,512]{0,3,2,1:T(8,128)(2,1)}, bf16[1024,6,1,512]{0,3,2,1:T(8,128)(2,1)}, bf16[1024,6,1,512]{0,3,2,1:T(8,128)(2,1)}) fusion(bf16[1024,6,3,512]{0,3,2,1:T(8,128)(2,1)} %bitcast.308), kind=kLoop, calls=%fused_computation.197 | loop fusion | bytes 37748736 | tf_op jit(solution)/shard_map/slice | solution.py:361
  251.6 2.4 fusion.101
  256.8 2.7 reshape.520
  259.6 3.2 copy.112
  262.7 2.5 mul.302
  265.3 5.3 copy.119
  270.6 3.9 copy.125
  281.1 41.0 %while.30 = (s32[]{:T(128)}, bf16[4,256,8,128]{1,3,2,0:T(8,128)(2,1)}, f32[4,8,256]{2,1,0:T(8,128)}, bf16[4,1280,256]{2,1,0:T(8,128)(2,1)}, s32[4,256]{1,0:T(4,1...) while((s32[]{:T(128)}, ...), condition=%wide.region_7.8_spmd.clone, body=%wide.region_4.7_spmd.clone.sunk | while | flops 1372978688 | bytes 53165240 | solution.py:494
  287.4 2.7 fusion.148
  297.6 2.7 fusion.148
  307.8 2.7 fusion.148
  318.0 2.7 fusion.148
  322.1 4.6 copy.113
  326.7 5.5 multiply_reduce_fusion.2
  332.8 9.3 %fusion.102 = f32[1024,3072]{1,0:T(8,128)} fusion(bf16[1024,1024]{1,0:T(8,128)(2,1)S(1)} %multiply_convert_fusion.1, bf16[1024,3072]{0,1:T(8,128)(2,1)S(1)} %bitcast.324), kind=kOutput, calls=%fused_computation.202 | convolution fusion | flops 6442450944 | bytes 20971520 | tf_op jit(solution)/shard_map/dot_general | solution.py:41
  342.2 9.6 %fusion.103 = f32[1024,3072]{1,0:T(8,128)} fusion(bf16[1024,1024]{1,0:T(8,128)(2,1)S(1)} %multiply_convert_fusion.1, bf16[1024,3072]{0,1:T(8,128)(2,1)S(1)} %bitcast.321), kind=kOutput, calls=%fused_computation.203 | convolution fusion | flops 6442450944 | bytes 20971520 | tf_op jit(solution)/shard_map/dot_general | solution.py:41
  351.8 23.5 %fusion.50 = (bf16[1024,3072]{1,0:T(8,128)(2,1)}, bf16[1024,3072]{1,0:T(8,128)(2,1)}, bf16[1024,3072]{1,0:T(8,128)(2,1)}) fusion(f32[1024,3072]{1,0:T(8,128)} %fusion.102, f32[1024,3072]{1,0:T(8,128)} %fusion.103, bf16[1024,3072]{0,1:T(8,128)(2,1)} %bitcast.327, bf16[1024,1024]{1,0:T(8,128)(2,1)S(1)} %bitcast.331), kind=kOutput, calls=%fused_computation.79 | convolution fusion | flops 6524239872 | bytes 52428800 | tf_op jit(solution)/shard_map/dot_general | solution.py:41
  375.3 11.7 %add_convert_fusion = bf16[1024,1024]{1,0:T(8,128)(2,1)} fusion(f32[1024,1024]{1,0:T(8,128)S(1)} %get-tuple-element.346, bf16[1024,3072]{1,0:T(8,128)(2,1)} %get-tuple-element.314, bf16[1024,3072]{0,1:T(8,128)(2,1)} %bitcast.328), kind=kOutput, calls=%fused_computation.115 | convolution fusion | flops 6444548096 | bytes 18874368 | tf_op jit(solution)/shard_map/dot_general | solution.py:51
  387.0 8.7 convolution_convert_fusion
  395.7 8.4 fusion.104
  404.1 8.9 convolution_convert_fusion.2
  413.0 2.3 reshape.542
  415.4 11.6 %convolution_convert_fusion.1 = bf16[1024,3072]{1,0:T(8,128)(2,1)} fusion(bf16[1024,1024]{1,0:T(8,128)(2,1)} %copy-done.28, bf16[1024,3072]{1,0:T(8,128)(2,1)} %get-tuple-element.312), kind=kOutput, calls=%fused_computation.86 | convolution fusion | flops 6445596672 | bytes 14680064 | tf_op jit(solution)/shard_map/dot_general | solution.py:45
  426.9 11.5 %multiply_reduce_fusion = (f32[1024]{0:T(1024)S(1)}, f32[1024]{0:T(1024)S(1)}, f32[1024,1024]{1,0:T(8,128)S(1)}) fusion(f32[1024,1024]{1,0:T(8,128)S(1)} %copy-done.13, f32[1024]{0:T(1024)S(1)} %fusion.89, f32[1024]{0:T(1024)S(1)} %bitcast.360, f32[1024,1024]{1,0:T(8,128)S(1)} %copy-done.46, bf16[1024,3072]{1,0:T(8,128)(2,1)} %get-tuple-element.312, ...), kind=kOutput, calls=%fused_computation.113 | convolution fusion | flops 6449788928 | bytes 25182208 | tf_op jit(solution)/shard_map/dot_general | solution.py:51
  439.7 2.5 convert_bitcast_fusion.1
  442.2 5.4 convert_bitcast_fusion
  448.2 115.4 %while.31 = (s32[]{:T(128)}, f32[4,256,8,128]{3,2,1,0:T(8,128)}, f32[4,1280,256]{1,2,0:T(8,128)}, bf16[4,1280,256]{2,1,0:T(8,128)(2,1)}, s32[4,256]{1,0:T(4,128)...) while((s32[]{:T(128)}, f32[4,256,8,128]{3,2,1,0:T(8,128)}, ...), condition=%wide.region_12.13_spmd.clone, body=%wide.region_10.12_spmd.clone.sunk | while | flops 3381755392 | bytes 189390160 | solution.py:519
  453.7 4.3 fusion.155
  466.7 6.4 fusion.158
  473.2 3.1 fusion.159
  482.5 4.3 fusion.155
  495.5 6.3 fusion.158
  501.9 3.1 fusion.159
  511.2 4.3 fusion.155
  524.2 6.4 fusion.158
  530.6 3.1 fusion.159
  539.9 4.3 fusion.155
  552.9 6.4 fusion.158
  559.4 3.1 fusion.159
  563.6 2.7 convert.35
  572.9 8.6 copy.129
  581.5 8.6 copy.128
  590.1 13.6 %pad_maximum_fusion.1 = bf16[1024,6,3,512]{0,3,1,2:T(8,128)(2,1)} fusion(bf16[1024,6,1,512]{0,3,1,2:T(8,128)(2,1)} %bitcast.326, bf16[1024,6,1,512]{0,3,1,2:T(8,128)(2,1)} %bitcast.312, bf16[1024,6,1,512]{0,3,1,2:T(8,128)(2,1)} %bitcast.313), kind=kLoop, calls=%fused_computation.67 | loop fusion | flops 18874368 | bytes 37748736 | tf_op jit(solution)/shard_map/stack | solution.py:355
  603.7 40.7 %copy.130 = bf16[1024,6,3,512]{3,2,1,0:T(4,128)(2,1)} copy(bf16[1024,6,3,512]{0,3,1,2:T(8,128)(2,1)} %pad_maximum_fusion.1) | data formatting | bytes 37748736 | tf_op jit(solution)/shard_map/stack | solution.py:355
  644.4 50.7 %concatenate.65 = bf16[2,2,4,2,32,9216]{5,4,3,2,1,0:T(8,128)(2,1)} reshape(bf16[1024,6,3,512]{3,2,1,0:T(4,128)(2,1)} %copy.130) | data formatting | bytes 37748736 | tf_op jit(solution)/shard_map/concatenate | solution.py:551
  695.2 2.7 copy.127
  697.9 6.0 fusion.75
  703.9 4.6 slice_negate_fusion
  711.5 4.7 maximum_multiply_fusion.1
  717.4 2.7 fusion.54
  720.2 7.7 fusion.60
  728.9 5.3 convolution_convert_fusion.3
  734.1 15.3 %pad_maximum_fusion.own_ref = bf16[2,2,4,2,32,11648]{5,4,3,2,1,0:T(8,128)(2,1)} fusion(bf16[2,2,4,2,32,9216]{5,4,3,2,1,0:T(8,128)(2,1)} %concatenate.65, bf16[2,2,4,2,32,1024]{5,4,3,2,1,0:T(8,128)(2,1)S(1)} %copy-done.24, bf16[2,2,4,2,32,128]{5,4,3,2,1,0:T(8,128)(2,1)S(1)} %bitcast.346, bf16[2,2,4,2,32,1280]{5,4,3,2,1,0:T(8,128)(2,1)S(1)} %convolution_convert_fusion.3), kind=kLoop, calls=%fused_computation.66 | loop fusion | flops 95420416 | bytes 47710208 | tf_op jit(solution)/shard_map/concatenate | solution.py:551
  749.5 121.9 %scatter_grads.1 = f32[32,11648]{1,0:T(8,128)} custom-call(bf16[2,2,4,2,32,11648]{5,4,3,2,1,0:T(8,128)(2,1)} %pad_maximum_fusion.own_ref), custom_call_target="tpu_custom_call" | custom-call | tf_op jit(solution)/shard_map/scatter_grads/pallas_call | solution.py:328
  879.1 6.1 slice_reduce_fusion
  888.2 3.9 fusion.53
  (340 shorter events, 150.6 us)
Async XLA Ops:
  0.6 10.1 %copy-start.43 = (bf16[32,128]{1,0:T(8,128)(2,1)S(1)}, bf16[32,128]{1,0:T(8,128)(2,1)}, u32[]{:S(2)}) copy-start(bf16[32,128]{1,0:T(8,128)(2,1)} %param.29) | copy-start | bytes 24580
  0.7 10.1 %copy-start.44 = (bf16[32,128]{1,0:T(8,128)(2,1)S(1)}, bf16[32,128]{1,0:T(8,128)(2,1)}, u32[]{:S(2)}) copy-start(bf16[32,128]{1,0:T(8,128)(2,1)} %param.30) | copy-start | bytes 24580
  0.7 10.3 %copy-start.36 = (bf16[1024,32]{0,1:T(8,128)(2,1)S(1)}, bf16[1024,32]{0,1:T(8,128)(2,1)}, u32[]{:S(2)}) copy-start(bf16[1024,32]{0,1:T(8,128)(2,1)} %param.31) | copy-start | bytes 196612
  11.9 119.3 %copy-start.5 = (bf16[4,256,1024]{2,1,0:T(8,128)(2,1)S(1)}, bf16[4,256,1024]{2,1,0:T(8,128)(2,1)}, u32[]{:S(2)}) copy-start(bf16[4,256,1024]{2,1,0:T(8,128)(2,1)} %param.24) | copy-start | bytes 6291460
  131.2 77.0 %copy-start.34 = (f32[1024,1]{0,1:T(1,128)}, f32[1024,1]{0,1:T(1,128)S(1)}, u32[]{:S(2)}) copy-start(f32[1024,1]{0,1:T(1,128)S(1)} %get-tuple-element.337) | copy-start | bytes 12292
  131.8 4.4 copy-start.41
  173.5 101.7 %collective-permute-start = (bf16[4,256,256]{2,1,0:T(8,128)(2,1)S(1)}, bf16[4,256,256]{2,1,0:T(8,128)(2,1)}, u32[]{:S(2)}, u32[]{:S(2)}) collective-permute-start(bf16[4,256,256]{2,1,0:T(8,128)(2,1)S(1)} %bitcast.338), channel_id=1, source_target_pairs={{0,4},{1,5},{2,6},{3,7},{8,12},{9,13},{10,14},{11,15},{16,20},{17,... | collective-permute-start | bytes 1572872 | tf_op jit(solution)/shard_map/ppermute | solution.py:411
  175.6 100.6 %collective-permute-start.1 = (bf16[4,256,256]{2,1,0:T(8,128)(2,1)S(1)}, bf16[4,256,256]{2,1,0:T(8,128)(2,1)}, u32[]{:S(2)}, u32[]{:S(2)}) collective-permute-start(bf16[4,256,256]{2,1,0:T(8,128)(2,1)S(1)} %bitcast.339), channel_id=1, source_target_pairs={{0,3},{1,4},{2,5},{3,6},{4,7},{8,11},{9,12},{10,13},{11,14},{12,15... | collective-permute-start | bytes 1572872 | tf_op jit(solution)/shard_map/ppermute | solution.py:411
  183.1 94.3 %collective-permute-start.2 = (bf16[4,256,256]{2,1,0:T(8,128)(2,1)S(1)}, bf16[4,256,256]{2,1,0:T(8,128)(2,1)}, u32[]{:S(2)}, u32[]{:S(2)}) collective-permute-start(bf16[4,256,256]{2,1,0:T(8,128)(2,1)S(1)} %bitcast.340), channel_id=1, source_target_pairs={{0,2},{1,3},{2,4},{3,5},{4,6},{5,7},{8,10},{9,11},{10,12},{11,13},... | collective-permute-start | bytes 1572872 | tf_op jit(solution)/shard_map/ppermute | solution.py:411
  185.2 93.3 %collective-permute-start.3 = (bf16[4,256,256]{2,1,0:T(8,128)(2,1)S(1)}, bf16[4,256,256]{2,1,0:T(8,128)(2,1)}, u32[]{:S(2)}, u32[]{:S(2)}) collective-permute-start(bf16[4,256,256]{2,1,0:T(8,128)(2,1)S(1)} %bitcast.341), channel_id=1, source_target_pairs={{0,1},{1,2},{2,3},{3,4},{4,5},{5,6},{6,7},{8,9},{9,10},{10,11},{11... | collective-permute-start | bytes 1572872 | tf_op jit(solution)/shard_map/ppermute | solution.py:411
  237.6 14.0 %copy-start.30 = (bf16[4,256,1024]{2,1,0:T(8,128)(2,1)S(1)}, bf16[4,256,1024]{2,1,0:T(8,128)(2,1)}, u32[]{:S(2)}) copy-start(bf16[4,256,1024]{2,1,0:T(8,128)(2,1)} %fusion.63) | copy-start | bytes 6291460
  284.6 2.8 copy-start.26
  294.8 2.8 copy-start.26
  315.2 2.8 copy-start.26
  322.1 10.2 %copy-start.2 = (bf16[4,256,8,128]{3,1,2,0:T(8,128)(2,1)}, bf16[4,256,8,128]{3,1,2,0:T(8,128)(2,1)S(1)}, u32[]{:S(2)}) copy-start(bf16[4,256,8,128]{3,1,2,0:T(8,128)(2,1)S(1)} %get-tuple-element.533) | copy-start | bytes 6291460
  322.1 10.2 %copy-start.33 = (s32[4,256]{1,0:T(4,128)}, s32[4,256]{1,0:T(4,128)S(1)}, u32[]{:S(2)}) copy-start(s32[4,256]{1,0:T(4,128)S(1)} %get-tuple-element.541) | copy-start | bytes 12292
  326.7 6.0 slice-start.4
  326.7 6.0 slice-start.5
  332.3 43.0 %copy-start.12 = (f32[1024,1024]{1,0:T(8,128)}, f32[1024,1024]{1,0:T(8,128)S(1)}, u32[]{:S(2)}) copy-start(f32[1024,1024]{1,0:T(8,128)S(1)} %get-tuple-element.346) | copy-start | bytes 12582916
  332.3 9.8 %slice-start.2 = ((s8[6291456]{0:T(1024)(128)(4,1)}), s8[4194304]{0:T(1024)(128)(4,1)S(1)}, s32[]{:S(2)}) async-start(s8[6291456]{0:T(1024)(128)(4,1)} %bitcast.319), calls=%async_computation.2 | async-start | bytes 8388608
  332.7 9.4 %copy-start.28 = (bf16[1024,1024]{1,0:T(8,128)(2,1)}, bf16[1024,1024]{1,0:T(8,128)(2,1)S(1)}, u32[]{:S(2)}) copy-start(bf16[1024,1024]{1,0:T(8,128)(2,1)S(1)} %multiply_convert_fusion.1) | copy-start | bytes 6291460
  332.8 9.4 %slice-start.3 = ((s8[6291456]{0:T(1024)(128)(4,1)}), s8[2097152]{0:T(1024)(128)(4,1)S(1)}, s32[]{:S(2)}) async-start(s8[6291456]{0:T(1024)(128)(4,1)} %bitcast.319), calls=%async_computation.3 | async-start | bytes 4194304
  342.1 9.6 %copy-start.22 = (bf16[4,256,1024]{2,1,0:T(8,128)(2,1)S(1)}, bf16[4,256,1024]{2,1,0:T(8,128)(2,1)}, u32[]{:S(2)}) copy-start(bf16[4,256,1024]{2,1,0:T(8,128)(2,1)} %param.26) | copy-start | bytes 6291460
  375.3 11.7 %copy-start.47 = (bf16[1024,3072]{1,0:T(8,128)(2,1)S(1)}, bf16[1024,3072]{1,0:T(8,128)(2,1)}, u32[]{:S(2)}) copy-start(bf16[1024,3072]{1,0:T(8,128)(2,1)} %get-tuple-element.314) | copy-start | bytes 18874372
  387.0 8.7 copy-start.45
  395.7 8.4 copy-start.29
  404.1 8.9 copy-start.17
  415.3 11.6 %copy-start.13 = (f32[1024,1024]{1,0:T(8,128)S(1)}, f32[1024,1024]{1,0:T(8,128)}, u32[]{:S(2)}) copy-start(f32[1024,1024]{1,0:T(8,128)} %copy-done.12) | copy-start | bytes 12582916
  415.4 11.6 %copy-start.46 = (f32[1024,1024]{1,0:T(8,128)S(1)}, f32[1024,1024]{1,0:T(8,128)}, u32[]{:S(2)}) copy-start(f32[1024,1024]{1,0:T(8,128)} %fusion.104) | copy-start | bytes 12582916
  426.9 12.8 %copy-start.23 = (bf16[4,256,1024]{2,1,0:T(8,128)(2,1)S(1)}, bf16[4,256,1024]{2,1,0:T(8,128)(2,1)}, u32[]{:S(2)}) copy-start(bf16[4,256,1024]{2,1,0:T(8,128)(2,1)} %param.26) | copy-start | bytes 6291460
  442.2 5.4 copy-start.10
  448.7 3.2 copy-start.14
  458.0 4.0 copy-start
  465.6 7.5 slice-start
  466.7 6.4 slice-start.1
  473.1 4.3 copy-start.15
  477.4 3.2 copy-start.14
  486.8 4.0 copy-start
  494.4 7.5 slice-start
  495.5 6.4 slice-start.1
  501.9 4.2 copy-start.15
  506.1 3.2 copy-start.14
  515.5 4.0 copy-start
  523.1 7.5 slice-start
  524.2 6.4 slice-start.1
  530.6 4.2 copy-start.15
  534.9 3.2 copy-start.14
  544.2 4.0 copy-start
  551.8 7.5 slice-start
  552.9 6.4 slice-start.1
  559.4 4.3 copy-start.15
  567.7 140.8 %collective-permute-start.7 = (bf16[4,256,256]{1,2,0:T(8,128)(2,1)}, bf16[4,256,256]{1,2,0:T(8,128)(2,1)S(1)}, u32[]{:S(2)}, u32[]{:S(2)}) collective-permute-start(bf16[4,256,256]{1,2,0:T(8,128)(2,1)} %get-tuple-element.323), channel_id=1, source_target_pairs={{4,0},{5,1},{6,2},{7,3},{12,8},{13,9},{14,10},{15,11},{20,16},{21,... | collective-permute-start | bytes 1572872 | tf_op jit(solution)/shard_map/ppermute | solution.py:411
  569.0 139.5 %collective-permute-start.6 = (bf16[4,256,256]{1,2,0:T(8,128)(2,1)}, bf16[4,256,256]{1,2,0:T(8,128)(2,1)}, u32[]{:S(2)}, u32[]{:S(2)}) collective-permute-start(bf16[4,256,256]{1,2,0:T(8,128)(2,1)} %get-tuple-element.324), channel_id=1, source_target_pairs={{3,0},{4,1},{5,2},{6,3},{7,4},{11,8},{12,9},{13,10},{14,11},{15,12... | collective-permute-start | bytes 1572872 | tf_op jit(solution)/shard_map/ppermute | solution.py:411
  570.3 138.2 %collective-permute-start.5 = (bf16[4,256,256]{1,2,0:T(8,128)(2,1)}, bf16[4,256,256]{1,2,0:T(8,128)(2,1)}, u32[]{:S(2)}, u32[]{:S(2)}) collective-permute-start(bf16[4,256,256]{1,2,0:T(8,128)(2,1)} %get-tuple-element.325), channel_id=1, source_target_pairs={{2,0},{3,1},{4,2},{5,3},{6,4},{7,5},{10,8},{11,9},{12,10},{13,11},... | collective-permute-start | bytes 1572872 | tf_op jit(solution)/shard_map/ppermute | solution.py:411
  571.6 137.0 %collective-permute-start.4 = (bf16[4,256,256]{1,2,0:T(8,128)(2,1)S(1)}, bf16[4,256,256]{1,2,0:T(8,128)(2,1)}, u32[]{:S(2)}, u32[]{:S(2)}) collective-permute-start(bf16[4,256,256]{1,2,0:T(8,128)(2,1)S(1)} %get-tuple-element.322), channel_id=1, source_target_pairs={{1,0},{2,1},{3,2},{4,3},{5,4},{6,5},{7,6},{9,8},{10,9},{11,10},{12... | collective-permute-start | bytes 1572872 | tf_op jit(solution)/shard_map/ppermute | solution.py:411
  644.4 50.7 %copy-start.16 = (bf16[1024,1024]{0,1:T(8,128)(2,1)S(1)}, bf16[1024,1024]{0,1:T(8,128)(2,1)}, u32[]{:S(2)}) copy-start(bf16[1024,1024]{0,1:T(8,128)(2,1)} %get-tuple-element.306) | copy-start | bytes 6291460
  697.8 6.0 copy-start.3
  711.5 4.8 copy-start.4
  711.5 5.9 copy-start.9
  720.1 7.8 copy-start.25
  720.2 8.4 copy-start.42
  728.8 5.3 copy-start.24
  749.5 127.8 %copy-start.40 = (f32[1,2,4,128]{3,1,2,0:T(2,128)S(1)}, f32[1,2,4,128]{3,1,2,0:T(2,128)}, u32[]{:S(2)}) copy-start(f32[1,2,4,128]{3,1,2,0:T(2,128)} %copy-done.39) | copy-start | bytes 12292
  879.1 9.1 %copy-start.11 = (f32[1024,1024]{1,0:T(8,128)S(1)}, f32[1024,1024]{1,0:T(8,128)}, u32[]{:S(2)}) copy-start(f32[1024,1024]{1,0:T(8,128)} %copy-done.10) | copy-start | bytes 12582916
  (22 other events, 43.1 us)

commit v2 on v1

--- a/solution.py
+++ b/solution.py
@@ -13,38 +13,18 @@
 MIB = 1 << 20
 
 
-def rotate(values, cosine, sine):
-    half_width = values.shape[-1] // 2
-    turned = jnp.concatenate([-values[..., half_width:], values[..., :half_width]], axis=-1)
-    return values * cosine + turned * sine
-
-
 def tables(positions, head_dim):
     inverse = 10000.0 ** (-2.0 * jnp.arange(head_dim // 2, dtype=jnp.float32) / head_dim)
     angle = positions.astype(jnp.float32)[:, None] * inverse[None, :]
     cosine, sine = jnp.cos(angle), jnp.sin(angle)
     return (
         jnp.concatenate([cosine, cosine], axis=-1),
-        jnp.concatenate([sine, sine], axis=-1),
-    )
-
-
-def rms_scale(values, gain):
-    return values * lax.rsqrt(jnp.mean(values * values, axis=-1, keepdims=True) + 1e-06) * gain
-
-
-def gated(gate, up_part):
-    return jax.nn.gelu(gate, approximate=True) * up_part
+        jnp.concatenate([-sine, sine], axis=-1),
+    )
 
 
 def matmul(left, right):
     return jnp.dot(left, right, preferred_element_type=jnp.float32)
-
-
-def left_times(left, right):
-    return lax.dot_general(
-        left, right, (((0,), (0,)), ((), ())), preferred_element_type=jnp.float32
-    )
 
 
 def right_times(left, right):
@@ -338,6 +318,457 @@
     )(own.reshape(2, 2, 4, 2, rows, columns))
 
 
+ROW_TILE = 256
+LOG2E = 1.4426950408889634
+NEG = -1e30
+
+
+def row(block, index):
+    return pl.BlockSpec(block, index)
+
+
+def vmem():
+    return pl.BlockSpec(memory_space=pltpu.VMEM)
+
+
+def hbm():
+    return pl.BlockSpec(memory_space=pl.ANY)
+
+
+def params(**more):
+    return pltpu.CompilerParams(vmem_limit_bytes=58 * MIB, **more)
+
+
+def inverse_rms(values):
+    return lax.rsqrt(jnp.mean(values * values, axis=-1, keepdims=True) + 1e-06)
+
+
+def rms_back(values, scale, gain, grad):
+    inner = jnp.mean(values * gain * grad, axis=-1, keepdims=True)
+    return scale * gain * grad - values * (scale * scale * scale * inner)
+
+
+def project_kernel(x_ref, cos_ref, sin_ref, w_ref, h_ref, q_ref, kv_ref, gains_ref):
+    heads, head_dim = q_ref.shape[1], q_ref.shape[3]
+    width = heads * head_dim
+    gains = w_ref[:, width + 2 * head_dim :].astype(jnp.float32).T[:8]
+
+    @pl.when(pl.program_id(0) == 0)
+    def _():
+        gains_ref[...] = gains
+
+    x = x_ref[...].astype(jnp.float32)
+    normed = (x * inverse_rms(x) * gains[0:1]).astype(jnp.bfloat16)
+    h_ref[...] = normed
+    cosine, sine = cos_ref[...], sin_ref[...]
+
+    def turn(u):
+        return (u * cosine + pltpu.roll(u, head_dim // 2, 1) * sine).astype(jnp.bfloat16)
+
+    for pair in range(heads // 2):
+        both = matmul(normed, w_ref[:, 2 * pair * head_dim : (2 * pair + 2) * head_dim])
+        q_ref[0, 2 * pair] = turn(both[:, :head_dim])
+        q_ref[0, 2 * pair + 1] = turn(both[:, head_dim:])
+    both = matmul(normed, w_ref[:, width : width + 2 * head_dim])
+    kv_ref[0, :, :head_dim] = turn(both[:, :head_dim])
+    kv_ref[0, :, head_dim:] = both[:, head_dim:].astype(jnp.bfloat16)
+
+
+def project(x, cosine, sine, weights, seqs, heads, head_dim):
+    rows, width = x.shape
+    block = rows // seqs
+    return pl.pallas_call(
+        project_kernel,
+        grid=(seqs,),
+        in_specs=[
+            row((block, width), lambda b: (b, 0)),
+            row((block, head_dim), lambda b: (b, 0)),
+            row((block, head_dim), lambda b: (b, 0)),
+            row(weights.shape, lambda b: (0, 0)),
+        ],
+        out_specs=[
+            row((block, width), lambda b: (b, 0)),
+            row((1, heads, block, head_dim), lambda b: (b, 0, 0, 0)),
+            row((1, block, 2 * head_dim), lambda b: (b, 0, 0)),
+            row((8, width), lambda b: (0, 0)),
+        ],
+        out_shape=[
+            jax.ShapeDtypeStruct((rows, width), jnp.bfloat16),
+            jax.ShapeDtypeStruct((seqs, heads, block, head_dim), jnp.bfloat16),
+            jax.ShapeDtypeStruct((seqs, block, 2 * head_dim), jnp.bfloat16),
+            jax.ShapeDtypeStruct((8, width), jnp.float32),
+        ],
+        compiler_params=params(),
+        name="project",
+    )(x, cosine, sine, weights)
+
+
+HALF = 128
+GROUP = 4
+
+
+def attend_kernel(scale, q_ref, kv_ref, low_ref, o_ref, lse_ref):
+    heads, block, head_dim = q_ref.shape[1:]
+    span = kv_ref.shape[1] - (block - HALF)
+    factor = scale * LOG2E
+
+    @pl.loop(0, block // HALF)
+    def _(half):
+        first = pl.multiple_of(half * HALF, HALF)
+        keys = kv_ref[0, pl.ds(first, span), :head_dim]
+        values = kv_ref[0, pl.ds(first, span), head_dim:]
+        values = jnp.concatenate([values, jnp.ones_like(values)], axis=1)
+        place = lax.broadcasted_iota(jnp.int32, (HALF, span), 1)
+        local = lax.broadcasted_iota(jnp.int32, (HALF, span), 0)
+        low = low_ref[0, pl.ds(first, HALF)] - first
+        allowed = (place >= low) & (place <= local + (span - HALF))
+        bias = jnp.where(allowed, 0.0, NEG)
+
+        @pl.loop(0, heads // GROUP)
+        def _(group):
+            base = group * GROUP
+            query = q_ref[0, pl.ds(base, GROUP), pl.ds(first, HALF)].reshape(
+                GROUP * HALF, head_dim
+            )
+            score = right_times(query, keys).reshape(GROUP, HALF, span) + bias[None]
+            peak = jnp.max(score, axis=-1, keepdims=True) * factor
+            weights = jnp.exp2(score * factor - peak).astype(jnp.bfloat16)
+            both = matmul(weights.reshape(GROUP * HALF, span), values)
+            total = both[:, head_dim:]
+            result = (both[:, :head_dim] / total).astype(jnp.bfloat16)
+            o_ref[0, pl.ds(base, GROUP), pl.ds(first, HALF)] = result.reshape(
+                GROUP, HALF, head_dim
+            )
+            log_total = jnp.log2(total) + peak.reshape(GROUP * HALF, 1)
+            lse_ref[0, half, group] = log_total.T[:8]
+
+
+def attend(query, pairs, low, scale):
+    seqs, heads, block, head_dim = query.shape
+    span = pairs.shape[1]
+    return pl.pallas_call(
+        functools.partial(attend_kernel, scale),
+        grid=(seqs,),
+        in_specs=[
+            row((1, heads, block, head_dim), lambda b: (b, 0, 0, 0)),
+            row((1, span, 2 * head_dim), lambda b: (b, 0, 0)),
+            row((1, block, 1), lambda b: (b, 0, 0)),
+        ],
+        out_specs=[
+            row((1, heads, block, head_dim), lambda b: (b, 0, 0, 0)),
+            row(
+                (1, block // HALF, heads // GROUP, 8, GROUP * HALF), lambda b: (b, 0, 0, 0, 0)
+            ),
+        ],
+        out_shape=[
+            jax.ShapeDtypeStruct(query.shape, jnp.bfloat16),
+            jax.ShapeDtypeStruct(
+                (seqs, block // HALF, heads // GROUP, 8, GROUP * HALF), jnp.float32
+            ),
+        ],
+        compiler_params=params(),
+        name="attend",
+    )(query, pairs, low[:, :, None])
+
+
+def attend_back_kernel(
+    scale, q_ref, kv_ref, low_ref, lse_ref, o_ref, do_ref, cos_ref, sin_ref, dq_ref, dkv_ref
+):
+    heads, block, head_dim = q_ref.shape[1:]
+    span = kv_ref.shape[1] - (block - HALF)
+    factor = scale * LOG2E
+    lanes = GROUP * HALF
+    dkv_ref[...] = jnp.zeros_like(dkv_ref)
+
+    @pl.loop(0, block // HALF)
+    def _(half):
+        first = pl.multiple_of(half * HALF, HALF)
+        window = pl.ds(first, span)
+        keys = kv_ref[0, window, :head_dim]
+        values = kv_ref[0, window, head_dim:]
+        keys_t = keys.T
+        place = lax.broadcasted_iota(jnp.int32, (span, HALF), 0)
+        local = lax.broadcasted_iota(jnp.int32, (span, HALF), 1)
+        low = low_ref[0, :, pl.ds(first, HALF)] - first
+        allowed = (place >= low) & (place <= local + (span - HALF))
+        bias = jnp.where(allowed, 0.0, NEG)
+        bias = jnp.concatenate([bias] * GROUP, axis=1)
+        cosine = cos_ref[pl.ds(first, HALF)][None]
+        sine = sin_ref[pl.ds(first, HALF)][None]
+
+        @pl.loop(0, heads // GROUP)
+        def _(group):
+            base = group * GROUP
+            here = (0, pl.ds(base, GROUP), pl.ds(first, HALF))
+            query = q_ref[here].reshape(lanes, head_dim)
+            grad = do_ref[here].reshape(lanes, head_dim)
+            mixed = o_ref[here].reshape(lanes, head_dim)
+            product = grad.astype(jnp.float32) * mixed.astype(jnp.float32)
+            delta = jnp.sum(product.T, axis=0, keepdims=True)
+            lse = lse_ref[0, half, group][0:1]
+            score = right_times(keys, query)
+            weights = jnp.exp2((score * factor - lse) + bias)
+            low_weights = weights.astype(jnp.bfloat16)
+            dkv_ref[0, window, head_dim:] += matmul(low_weights, grad)
+            slope = right_times(values, grad)
+            slope = (weights * (slope - delta)).astype(jnp.bfloat16)
+            dkv_ref[0, window, :head_dim] += matmul(slope, query) * scale
+            dq = (matmul(keys_t, slope).T * scale).reshape(GROUP, HALF, head_dim)
+            turned = pltpu.roll(dq.reshape(lanes, head_dim), head_dim // 2, 1)
+            dq = dq * cosine - turned.reshape(GROUP, HALF, head_dim) * sine
+            dq_ref[here] = dq.astype(jnp.bfloat16)
+
+
+def attend_back(query, pairs, low, lse, mixed, grad, cosine, sine, scale):
+    seqs, heads, block, head_dim = query.shape
+    span = pairs.shape[1]
+    per_head = row((1, heads, block, head_dim), lambda b: (b, 0, 0, 0))
+    table = row((block, head_dim), lambda b: (b, 0))
+    return pl.pallas_call(
+        functools.partial(attend_back_kernel, scale),
+        grid=(seqs,),
+        in_specs=[
+            per_head,
+            row((1, span, 2 * head_dim), lambda b: (b, 0, 0)),
+            row((1, 1, block), lambda b: (b, 0, 0)),
+            row((1,) + lse.shape[1:], lambda b: (b, 0, 0, 0, 0)),
+            per_head,
+            per_head,
+            table,
+            table,
+        ],
+        out_specs=[per_head, row((1, span, 2 * head_dim), lambda b: (b, 0, 0))],
+        out_shape=[
+            jax.ShapeDtypeStruct(query.shape, jnp.bfloat16),
+            jax.ShapeDtypeStruct(pairs.shape, jnp.float32),
+        ],
+        compiler_params=params(),
+        name="attend_back",
+    )(query, pairs, low[:, None, :], lse, mixed, grad, cosine, sine)
+
+
+def gelu_parts(gate):
+    cube = 0.044715 * gate * gate
+    bend = jnp.tanh(0.7978845608028654 * gate * (1.0 + cube))
+    half = 0.5 * (1.0 + bend)
+    value = gate * half
+    slope = half + gate * (half * (1.0 - bend)) * (0.7978845608028654 * (1.0 + 3.0 * cube))
+    return value, slope
+
+
+def feed_kernel(
+    start,
+    x_ref,
+    o_ref,
+    g_ref,
+    gains_ref,
+    full_ref,
+    y_ref,
+    dx_ref,
+    do_ref,
+    dgain_ref,
+    dout_ref,
+    dff_ref,
+    outw,
+    ff,
+    mixed,
+    normed,
+    normed_t,
+    g_t,
+    y_acc,
+    dh_acc,
+    m_all,
+    dgate_all,
+    dup_all,
+    grads,
+    in_sem,
+    out_sem,
+):
+    rows, width = x_ref.shape
+    seqs, heads, block, head_dim = o_ref.shape
+    step = ff.shape[2] // 3
+    tiles = rows // ROW_TILE
+    gain = gains_ref[1:2]
+
+    def load(chunk):
+        return pltpu.make_async_copy(
+            full_ref.at[:, pl.ds(start + width + chunk * 3 * step, 3 * step)],
+            ff.at[chunk % 2],
+            in_sem.at[chunk % 2],
+        )
+
+    out_load = pltpu.make_async_copy(full_ref.at[:, pl.ds(start, width)], outw, in_sem.at[2])
+    out_load.start()
+    load(0).start()
+    out_load.wait()
+
+    def here(tile):
+        return pl.ds(pl.multiple_of(tile * ROW_TILE, ROW_TILE), ROW_TILE)
+
+    @pl.loop(0, tiles)
+    def _(tile):
+        part = here(tile)
+        attended = jnp.concatenate([o_ref[tile, h] for h in range(heads)], axis=1)
+        x1 = x_ref[part].astype(jnp.float32) + right_times(attended, outw[...])
+        mixed[part] = x1
+        y_acc[part] = x1
+        low = (x1 * inverse_rms(x1) * gain).astype(jnp.bfloat16)
+        normed[part] = low
+        normed_t[:, part] = low.T
+        g_t[:, part] = g_ref[part].T
+        dh_acc[part] = jnp.zeros((ROW_TILE, width), jnp.float32)
+
+    for chunk in range(FF_CHUNKS):
+        slot = chunk % 2
+        load(chunk).wait()
+        if chunk + 1 < FF_CHUNKS:
+            load(chunk + 1).start()
+
+        @pl.loop(0, tiles)
+        def _(tile):
+            part = here(tile)
+            low, grad = normed[part], g_ref[part]
+            gate = matmul(low, ff[slot, :, :step])
+            up_part = matmul(low, ff[slot, :, step : 2 * step])
+            dm = matmul(grad, ff[slot, :, 2 * step :])
+            value, slope = gelu_parts(gate)
+            m = (value * up_part).astype(jnp.bfloat16)
+            dgate = (dm * up_part * slope).astype(jnp.bfloat16)
+            dup = (dm * value).astype(jnp.bfloat16)
+            m_all[part], dgate_all[part], dup_all[part] = m, dgate, dup
+            y_acc[part] += right_times(m, ff[slot, :, 2 * step :])
+            dh_acc[part] += right_times(dgate, ff[slot, :, :step]) + right_times(
+                dup, ff[slot, :, step : 2 * step]
+            )
+
+        if chunk >= 2:
+            pltpu.make_async_copy(grads.at[slot], dff_ref.at[chunk - 2], out_sem.at[slot]).wait()
+
+        @pl.loop(0, width // ROW_TILE)
+        def _(tile):
+            part = here(tile)
+            grads[slot, part, :step] = matmul(normed_t[part], dgate_all[...]).astype(jnp.bfloat16)
+            grads[slot, part, step : 2 * step] = matmul(normed_t[part], dup_all[...]).astype(
+                jnp.bfloat16
+            )
+            grads[slot, part, 2 * step :] = matmul(g_t[part], m_all[...]).astype(jnp.bfloat16)
+
+        pltpu.make_async_copy(grads.at[slot], dff_ref.at[chunk], out_sem.at[slot]).start()
+
+    dgain_ref[...] = jnp.zeros_like(dgain_ref)
+
+    @pl.loop(0, tiles)
+    def _(tile):
+        part = here(tile)
+        y_ref[part] = y_acc[part].astype(jnp.bfloat16)
+        x1, dh = mixed[part], dh_acc[part]
+        scale = inverse_rms(x1)
+        dgain_ref[0:1] += jnp.sum(dh * x1 * scale, axis=0, keepdims=True)
+        dx = g_ref[part].astype(jnp.float32) + rms_back(x1, scale, gain, dh)
+        dx_ref[part] = dx
+        low = dx.astype(jnp.bfloat16)
+        g_t[:, part] = low.T
+        back = matmul(low, outw[...]).astype(jnp.bfloat16)
+        for h in range(heads):
+            do_ref[tile, h] = back[:, h * head_dim : (h + 1) * head_dim]
+
+    @pl.loop(0, width // ROW_TILE)
+    def _(tile):
+        part = here(tile)
+        for h in range(heads):
+            if h % 2 == 0:
+                for s in range(seqs):
+                    pair = jnp.concatenate([o_ref[s, h], o_ref[s, h + 1]], axis=1)
+                    term = matmul(g_t[part, s * block : (s + 1) * block], pair)
+                    total = term if s == 0 else total + term
+                dout_ref[part, h * head_dim : (h + 2) * head_dim] = total.astype(jnp.bfloat16)
+
+    for chunk in (FF_CHUNKS - 2, FF_CHUNKS - 1):
+        pltpu.make_async_copy(grads.at[chunk % 2], dff_ref.at[chunk], out_sem.at[chunk % 2]).wait()
+
+
+def feed(x, mixed_heads, grad, gains, full, start, hidden):
+    rows, width = x.shape
+    step = hidden // FF_CHUNKS
+    low = jnp.bfloat16
+    return pl.pallas_call(
+        functools.partial(feed_kernel, start),
+        in_specs=[vmem(), vmem(), vmem(), vmem(), hbm()],
+        out_specs=[vmem(), vmem(), vmem(), vmem(), vmem(), hbm()],
+        out_shape=[
+            jax.ShapeDtypeStruct((rows, width), low),
+            jax.ShapeDtypeStruct((rows, width), jnp.float32),
+            jax.ShapeDtypeStruct(mixed_heads.shape, low),
+            jax.ShapeDtypeStruct((8, width), jnp.float32),
+            jax.ShapeDtypeStruct((width, width), low),
+            jax.ShapeDtypeStruct((FF_CHUNKS, width, 3 * step), low),
+        ],
+        scratch_shapes=[
+            pltpu.VMEM((width, width), low),
+            pltpu.VMEM((2, width, 3 * step), low),
+            pltpu.VMEM((rows, width), jnp.float32),
+            pltpu.VMEM((rows, width), low),
+            pltpu.VMEM((width, rows), low),
+            pltpu.VMEM((width, rows), low),
+            pltpu.VMEM((rows, width), jnp.float32),
+            pltpu.VMEM((rows, width), jnp.float32),
+            pltpu.VMEM((rows, step), low),
+            pltpu.VMEM((rows, step), low),
+            pltpu.VMEM((rows, step), low),
+            pltpu.VMEM((2, width, 3 * step), low),
+            pltpu.SemaphoreType.DMA((3,)),
+            pltpu.SemaphoreType.DMA((2,)),
+        ],
+        compiler_params=params(),
+        name="feed",
+    )(x, mixed_heads, grad, gains, full)
+
+
+def finish_kernel(x_ref, h_ref, dq_ref, dkv_ref, gains_ref, dx_ref, w_ref, dw_ref, dxo_ref, dgain_ref, h_t, dall):
+    rows, width = x_ref.shape
+    seqs, heads, block, head_dim = dq_ref.shape
+    gain = gains_ref[0:1]
+    dgain_ref[...] = jnp.zeros_like(dgain_ref)
+
+    @pl.loop(0, seqs)
+    def _(tile):
+        part = pl.ds(pl.multiple_of(tile * block, block), block)
+        h_t[:, part] = h_ref[part].T
+        grad = jnp.concatenate([dq_ref[tile, h] for h in range(heads)] + [dkv_ref[tile]], axis=1)
+        dall[part] = grad
+        dh = right_times(grad, w_ref[:, : width + 2 * head_dim])
+        x = x_ref[part].astype(jnp.float32)
+        scale = inverse_rms(x)
+        dgain_ref[0:1] += jnp.sum(dh * x * scale, axis=0, keepdims=True)
+        dxo_ref[part] = (dx_ref[part] + rms_back(x, scale, gain, dh)).astype(jnp.bfloat16)
+
+    @pl.loop(0, width // ROW_TILE)
+    def _(tile):
+        part = pl.ds(pl.multiple_of(tile * ROW_TILE, ROW_TILE), ROW_TILE)
+        dw_ref[part] = matmul(h_t[part], dall[...]).astype(jnp.bfloat16)
+
+
+def finish(x, normed, dq, dkv, gains, dx, weights):
+    rows, width = x.shape
+    columns = width + dkv.shape[2]
+    return pl.pallas_call(
+        finish_kernel,
+        in_specs=[vmem()] * 7,
+        out_specs=[vmem()] * 3,
+        out_shape=[
+            jax.ShapeDtypeStruct((width, columns), jnp.bfloat16),
+            jax.ShapeDtypeStruct((rows, width), jnp.bfloat16),
+            jax.ShapeDtypeStruct((8, width), jnp.float32),
+        ],
+        scratch_shapes=[
+            pltpu.VMEM((width, rows), jnp.bfloat16),
+            pltpu.VMEM((rows, columns), jnp.bfloat16),
+        ],
+        compiler_params=params(),
+        name="finish",
+    )(x, normed, dq, dkv, gains, dx, weights)
+
+
 def columns_of(width, head_dim, heads, hidden):
     attention = width + 2 * head_dim + 128
     chunks = [(0, 640, attention), (attention, attention + width // 2, attention + width)]
@@ -359,50 +790,6 @@
     rows, hidden = stacked.shape[0], stacked.shape[1] // 3
     parts = stacked.reshape(rows, FF_CHUNKS, 3, hidden // FF_CHUNKS)
     return [parts[:, :, i].reshape(rows, hidden) for i in range(3)]
-
-
-def allowed_pairs(query_place, key_place, starts):
-    later = key_place[None, :] <= query_place[:, None]
-    inside = query_place[:, None] - key_place[None, :] < WINDOW
-    same_doc = key_place[None, :] >= starts[:, None]
-    return later & inside & same_doc
-
-
-def attend_one(query, pairs, starts, query_place, key_place, scale, head_dim):
-    keys = pairs[:, :head_dim]
-    values = pairs[:, head_dim:]
-    allowed = allowed_pairs(query_place, key_place, starts)
-    score = jnp.einsum("qhd,kd->hqk", query, keys, preferred_element_type=jnp.float32) * scale
-    score = jnp.where(allowed[None], score, -1e30)
-    peak = jnp.max(score, axis=-1, keepdims=True)
-    log_total = peak + jnp.log(jnp.sum(jnp.exp(score - peak), axis=-1, keepdims=True))
-    weights_low = jnp.exp(score - log_total).astype(jnp.bfloat16)
-    result = jnp.einsum("hqk,kd->qhd", weights_low, values, preferred_element_type=jnp.float32)
-    return (result, log_total[..., 0])
-
-
-def attend_back(query, pairs, starts, log_total, grad_out, query_place, key_place, scale, head_dim):
-    keys = pairs[:, :head_dim]
-    values = pairs[:, head_dim:]
-    allowed = allowed_pairs(query_place, key_place, starts)
-    score = jnp.einsum("qhd,kd->hqk", query, keys, preferred_element_type=jnp.float32) * scale
-    score = jnp.where(allowed[None], score, -1e30)
-    weights = jnp.exp(score - log_total[..., None])
-    weights_low = weights.astype(jnp.bfloat16)
-    grad_weights = jnp.einsum("qhd,kd->hqk", grad_out, values, preferred_element_type=jnp.float32)
-    grad_values = jnp.einsum(
-        "hqk,qhd->kd", weights_low, grad_out, preferred_element_type=jnp.float32
-    )
-    grad_score = (
-        weights * (grad_weights - jnp.sum(weights * grad_weights, axis=-1, keepdims=True))
-    ).astype(jnp.bfloat16)
-    grad_query = (
-        jnp.einsum("hqk,kd->qhd", grad_score, keys, preferred_element_type=jnp.float32) * scale
-    )
-    grad_keys = (
-        jnp.einsum("hqk,qhd->kd", grad_score, query, preferred_element_type=jnp.float32) * scale
-    )
-    return (grad_query, jnp.concatenate([grad_keys, grad_values], axis=-1))
 
 
 def shifted(value, axis, steps):
@@ -455,76 +842,25 @@
     else:
         full = lax.all_gather(shard, ("batch", "seq"), axis=0, tiled=True)
     all_segments = lax.all_gather(segments, "seq", axis=1, tiled=True)
-    query_full = full[:, :width]
-    key_full = full[:, width : width + head_dim]
-    value_full = full[:, width + head_dim : width + 2 * head_dim]
-    gains_full = full[:, width + 2 * head_dim : chunks[0][2]].astype(jnp.float32)
-    gain_one, gain_two = gains_full[:, 0], gains_full[:, 1]
-    out_t = full[:, chunks[1][0] : chunks[1][2]]
-    gate_full, up_full, down_t = unstack_ff(full[:, chunks[2][0] :])
-
     starts = jnp.sum(all_segments[:, None, :] < segments[:, :, None], axis=-1, dtype=jnp.int32)
     query_place = jnp.arange(block_len, dtype=jnp.int32) + lax.axis_index("seq") * block_len
-    key_place = query_place[0] - reach * block_len + jnp.arange(span, dtype=jnp.int32)
+    low = jnp.maximum(starts, query_place[None, :] - (WINDOW - 1))
+    low = low - (query_place[0] - reach * block_len)
     cosine, sine = tables((query_place[None, :] - starts).reshape(-1), head_dim)
 
-    def forward_item(item):
-        return attend_one(item[0], item[1], item[2], query_place, key_place, scale, head_dim)
-
-    def backward_item(item):
-        return attend_back(
-            item[0], item[1], item[2], item[3], item[4], query_place, key_place, scale, head_dim
-        )
-
-    inputs = tokens.reshape(rows, width).astype(jnp.float32)
-    normed_one = rms_scale(inputs, gain_one).astype(jnp.bfloat16)
-    query = rotate(
-        matmul(normed_one, query_full).reshape(rows, heads, head_dim),
-        cosine[:, None, :],
-        sine[:, None, :],
-    ).astype(jnp.bfloat16)
-    key_rot = rotate(matmul(normed_one, key_full), cosine, sine).astype(jnp.bfloat16)
-    value_low = matmul(normed_one, value_full).astype(jnp.bfloat16)
-    own_pairs = jnp.concatenate([key_rot, value_low], axis=-1).reshape(
-        seqs, block_len, 2 * head_dim
+    inputs = tokens.reshape(rows, width)
+    qkv_weights = full[:, : chunks[0][2]]
+    normed, query, own_pairs, gains = project(
+        inputs, cosine, sine, qkv_weights, seqs, heads, head_dim
     )
     pieces = [shifted(own_pairs, "seq", distance) for distance in range(reach, 0, -1)]
     window_pairs = jnp.concatenate(pieces + [own_pairs], axis=1)
-    query_seq = query.reshape(seqs, block_len, heads, head_dim)
-    attended, log_total = lax.map(forward_item, (query_seq, window_pairs, starts))
-    attended_low = attended.reshape(rows, heads * head_dim).astype(jnp.bfloat16)
-    mixed = inputs + right_times(attended_low, out_t)
-    normed_two = rms_scale(mixed, gain_two).astype(jnp.bfloat16)
-    gate = matmul(normed_two, gate_full)
-    up_part = matmul(normed_two, up_full)
-    hidden = gated(gate, up_part).astype(jnp.bfloat16)
-    output = (mixed + right_times(hidden, down_t)).astype(jnp.bfloat16)
-
-    grad_rows = cotangent.reshape(rows, width)
-    grad_down_t = left_times(grad_rows, hidden)
-    grad_hidden = matmul(grad_rows, down_t)
-    _, pull_gated = jax.vjp(gated, gate, up_part)
-    grad_gate, grad_up = pull_gated(grad_hidden)
-    grad_gate = grad_gate.astype(jnp.bfloat16)
-    grad_up = grad_up.astype(jnp.bfloat16)
-    grad_gate_w = left_times(normed_two, grad_gate)
-    grad_up_w = left_times(normed_two, grad_up)
-    grad_normed_two = right_times(grad_gate, gate_full) + right_times(grad_up, up_full)
-    _, pull_second = jax.vjp(rms_scale, mixed, gain_two)
-    grad_mixed, grad_gain_two = pull_second(grad_normed_two)
-    grad_mixed = grad_mixed + grad_rows.astype(jnp.float32)
-    grad_branch = grad_mixed.astype(jnp.bfloat16)
-    grad_out_t = left_times(grad_branch, attended_low)
-    grad_attended = matmul(grad_branch, out_t).astype(jnp.bfloat16)
-    grad_query, grad_pairs = lax.map(
-        backward_item,
-        (
-            query_seq,
-            window_pairs,
-            starts,
-            log_total,
-            grad_attended.reshape(seqs, block_len, heads, head_dim),
-        ),
+    mixed, log_total = attend(query, window_pairs, low, scale)
+    output, grad_mixed, grad_heads, grad_gain_two, grad_out_t, grad_ff = feed(
+        inputs, mixed, cotangent.reshape(rows, width), gains, full, chunks[1][0], hidden_width
+    )
+    grad_query, grad_pairs = attend_back(
+        query, window_pairs, low, log_total, mixed, grad_heads, cosine, sine, scale
     )
     own_grad = grad_pairs[:, reach * block_len :]
     for distance in range(1, reach + 1):
@@ -532,31 +868,18 @@
         own_grad = own_grad + shifted(piece.astype(jnp.bfloat16), "seq", -distance).astype(
             piece.dtype
         )
-    grad_key_rot = own_grad[..., :head_dim].reshape(rows, head_dim)
-    grad_value = own_grad[..., head_dim:].reshape(rows, head_dim).astype(jnp.bfloat16)
-    grad_q = rotate(
-        grad_query.reshape(rows, heads, head_dim), cosine[:, None, :], -sine[:, None, :]
-    )
-    grad_q = grad_q.reshape(rows, heads * head_dim).astype(jnp.bfloat16)
-    grad_k = rotate(grad_key_rot, cosine, -sine).astype(jnp.bfloat16)
-    grad_qkv = jnp.concatenate([grad_q, grad_k, grad_value], axis=1)
-    grad_qkv_w = left_times(normed_one, grad_qkv)
-    grad_normed_one = right_times(grad_qkv, full[:, : width + 2 * head_dim])
-    _, pull_first = jax.vjp(rms_scale, inputs, gain_one)
-    grad_x, grad_gain_one = pull_first(grad_normed_one)
-    grad_input = (grad_x + grad_mixed).astype(jnp.bfloat16)
-
-    grad_gains = jnp.zeros((width, 128), jnp.float32)
-    grad_gains = grad_gains.at[:, 0].set(grad_gain_one).at[:, 1].set(grad_gain_two)
-    grads = jnp.concatenate(
-        [
-            grad_qkv_w,
-            grad_gains,
-            grad_out_t,
-            stack_ff(grad_gate_w, grad_up_w, grad_down_t),
-        ],
-        axis=1,
+    grad_key = own_grad[..., :head_dim].reshape(rows, head_dim)
+    grad_key = grad_key * cosine - jnp.roll(grad_key, head_dim // 2, axis=1) * sine
+    grad_kv = jnp.concatenate(
+        [grad_key.reshape(seqs, block_len, head_dim), own_grad[..., head_dim:]], axis=-1
     ).astype(jnp.bfloat16)
+    grad_qkv_w, grad_input, grad_gain_one = finish(
+        inputs, normed, grad_query, grad_kv, gains, grad_mixed, qkv_weights
+    )
+    grad_gains = jnp.zeros((width, 128), jnp.bfloat16)
+    grad_gains = grad_gains.at[:, 0].set(grad_gain_one[0].astype(jnp.bfloat16))
+    grad_gains = grad_gains.at[:, 1].set(grad_gain_two[0].astype(jnp.bfloat16))
+    grads = jnp.concatenate([grad_qkv_w, grad_gains, grad_out_t] + list(grad_ff), axis=1)
     if own_links:
         share = scatter_all(grads, shard_rows, chunks)
     else:

time: 907 us -> 658 us (0.73)
  matrix products: 222 us -> 0 us
  local copies, waits for them, and re-layouts: 279 us -> 59.5 us
  Pallas kernels: 240 us -> 427 us
  waiting for transfers between devices: 0.02 us -> 87.6 us
  other arithmetic: 95.1 us -> 22.2 us
    dot_general x45 -> x0, matrix products: 222 us -> none  [the longest x7 54.1 us: matmul(): return jnp.dot(left, right, preferred_element_type=jnp.float32)]
    pallas_call x0 -> x5, Pallas kernels: none -> 176 us  [the longest x1 90.3 us: feed(): pl.pallas_call(functools.partial(feed_kernel, start), in_specs=[vmem(), v...]
    ppermute x8, waiting for transfers between devices: 0.02 us -> 87.6 us  [shifted(): lax.ppermute(value, axis, [(source, source + steps) for source in range(i...]
    concatenate x1, local copies, waits for them, and re-layouts: 50.7 us -> 1.91 us  [on_device(): jnp.concatenate([grad_qkv_w, grad_gains, grad_out_t] + list(grad_ff), axi...]
    another operation x5 -> x4, local copies, waits for them, and re-layouts: 44.7 us -> 4.03 us  [stack_ff(): return jnp.stack(parts, axis=2).reshape(rows, 3 * hidden)]
    while x64 -> x0, local copies, waits for them, and re-layouts: 22.4 us -> none
    convert_element_type x10 -> x1, other arithmetic: 18.9 us -> 0.01 us  [tables(): angle = positions.astype(jnp.float32)[:, None] * inverse[None, :]]
    slice x2 -> x1, local copies, waits for them, and re-layouts: 20.2 us -> 3.1 us  [unstack_ff(): return [parts[:, :, i].reshape(rows, hidden) for i in range(3)]]
  transfers between devices with their start and end apart: 8 -> 8, of which waited for: 0 -> 3; matrix products, arithmetic and copies ran while one was open for 25% -> 3% of each run, Pallas kernels for 0% -> 0%
where the time goes in v2:
time: 658 us; the launch traced here: 650 us
  Pallas kernels  427 us (65%)
  waiting for transfers between devices  87.6 us (13%)
  local copies, waits for them, and re-layouts  59.5 us (9%)
  blocking collectives  32.3 us (5%)
  other arithmetic  22.2 us (3%)
  starting transfers between devices  19.2 us (3%)
    pallas_call x1, Pallas kernels, scatter_all(): pl.pallas_call(functools.partial(scatter_kernel, chunks), out_shape=jax.S...  137 us
    pallas_call x1, Pallas kernels, gather_all(): pl.pallas_call(functools.partial(gather_kernel, chunks), out_shape=jax.Sh...  113 us
    pallas_call x1, Pallas kernels, feed(): pl.pallas_call(functools.partial(feed_kernel, start), in_specs=[vmem(), v...  90.3 us
    ppermute x8, waiting for transfers between devices, shifted(): lax.ppermute(value, axis, [(source, source + steps) for source in range(i...  87.6 us
    pallas_call x1, Pallas kernels, attend_back(): pl.pallas_call(functools.partial(attend_back_kernel, scale), grid=(seqs,)...  32.9 us
    all_gather x1, blocking collectives, on_device(): all_segments = lax.all_gather(segments, 'seq', axis=1, tiled=True)  32.3 us
    pallas_call x1, Pallas kernels, attend(): pl.pallas_call(functools.partial(attend_kernel, scale), grid=(seqs,), in_...  30.5 us
    unnamed x55, local copies, waits for them, and re-layouts  25.6 us
  transfers between devices with their start and end apart: 8, of which 3 were waited for; matrix products, arithmetic and copies ran while one was open for 3% of the time, Pallas kernels for 0%

profile of v2, /device:TPU:0, one launch (start us, length us, event | category | flops | bytes accessed | tf_op | source)
XLA Modules:
  0.0 649.8 jit_solution(4033752081852099885)
XLA Ops:
  0.7 0.6 compare_reduce_fusion.1
  1.3 0.6 compare_reduce_fusion
  2.0 1.3 fusion.7
  3.4 1.3 fusion.6
  4.8 32.3 %all_gather.3 = s32[4,2048]{1,0:T(4,128)S(1)} all-gather(s32[4,256]{1,0:T(4,128)} %param.21), channel_id=1, replica_groups=mesh['batch'=4,'seq'=8] {'seq'}, dimensions={1}, use_global_device_ids=true | all-gather | bytes 36864 | tf_op jit(solution)/shard_map/all_gather | solution.py:844
  37.1 1.7 convert_reduce_fusion
  38.8 1.2 stack_reshape.9
  40.0 1.2 stack_reshape.10
  41.2 1.2 stack_reshape.11
  43.1 0.8 reshape.313
  44.2 0.9 copy-done.11
  45.1 113.5 %gather_weights.1 = bf16[2,2,4,2,32,11648]{5,4,3,2,1,0:T(8,128)(2,1)} custom-call(bf16[32,11648]{1,0:T(8,128)(2,1)} %copy-done.11), custom_call_target="tpu_custom_call" | custom-call | tf_op jit(solution)/shard_map/gather_weights/pallas_call | solution.py:153
  158.6 3.6 slice.159.w_ref
  162.2 1.9 fusion.2
  164.1 1.3 pad_maximum_fusion.1
  165.4 8.1 %project.1 = (bf16[1024,1024]{1,0:T(8,128)(2,1)}, bf16[4,8,256,128]{3,2,1,0:T(8,128)(2,1)}, bf16[4,256,256]{2,1,0:T(8,128)(2,1)}, f32[8,1024]{1,0:T(8,128)}) custom-call(bf16[1024,1024]{1,0:T(8,128)(2,1)} %bitcast.45, f32[1024,128]{1,0:T(8,128)} %get-tuple-element.120.cos_ref, f32[1024,128]{1,0:T(8,128)} %get-tuple-element.121.sin_ref, ...), custom_call_target="tpu_custom_call" | custom-call | tf_op jit(solution)/shard_map/project/pallas_call | solution.py:380
  173.5 4.2 collective-permute-start.3
  177.7 7.0 %collective-permute-start.2 = (bf16[4,256,256]{2,1,0:T(8,128)(2,1)}, bf16[4,256,256]{2,1,0:T(8,128)(2,1)S(1)}, u32[]{:S(2)}, u32[]{:S(2)}) collective-permute-start(bf16[4,256,256]{2,1,0:T(8,128)(2,1)} %get-tuple-element.77), channel_id=1, source_target_pairs={{0,2},{1,3},{2,4},{3,5},{4,6},{5,7},{8,10},{9,11},{10,12},{11,13},... | collective-permute-start | bytes 1572872 | tf_op jit(solution)/shard_map/ppermute | solution.py:798
  184.7 1.4 collective-permute-start.1
  186.1 1.5 collective-permute-start
  187.6 3.2 fusion.3
  192.2 1.0 maximum_subtract_fusion.low_ref
  193.1 0.6 maximum_subtract_fusion.1.low_ref
  193.7 25.3 %collective-permute-done = bf16[4,256,256]{2,1,0:T(8,128)(2,1)S(1)} collective-permute-done((bf16[4,256,256]{2,1,0:T(8,128)(2,1)}, bf16[4,256,256]{2,1,0:T(8,128)(2,1)S(1)}, u32[]{:S(2)}, u32[]{:S(2)}) %collective-permute-start) | collective-permute-done | bytes 524320 | tf_op jit(solution)/shard_map/ppermute | solution.py:798
  219.3 1.5 copy-done
  220.9 30.5 %attend.1 = (bf16[4,8,256,128]{3,2,1,0:T(8,128)(2,1)}, f32[4,2,2,8,512]{4,3,2,1,0:T(8,128)}) custom-call(bf16[4,8,256,128]{3,2,1,0:T(8,128)(2,1)} %get-tuple-element.76.q_ref, bf16[4,1280,256]{2,1,0:T(8,128)(2,1)} %copy-done, s32[4,256,1]{2,1,0:T(8,128)} %maximum_subtract_fusion.low_ref), custom_call_target="tpu_custom_call" | custom-call | tf_op jit(solution)/shard_map/attend/pallas_call | solution.py:449
  251.4 90.3 %feed.1 = (bf16[1024,1024]{1,0:T(8,128)(2,1)}, f32[1024,1024]{1,0:T(8,128)}, bf16[4,8,256,128]{3,2,1,0:T(8,128)(2,1)}, f32[8,1024]{1,0:T(8,128)}, bf16[1024,1024...) custom-call(bf16[1024,1024]{1,0:T(8,128)(2,1)} %bitcast.46, bf16[4,8,256,128]{3,2,1,0:T(8,128)(2,1)} %get-tuple-element.78.o_ref, ...), custom_call_target="tpu_custom_call" | custom-call | tf_op jit(solution)/shard_map/feed/pallas_call | solution.py:694
  341.7 32.9 %attend_back.1 = (bf16[4,8,256,128]{3,2,1,0:T(8,128)(2,1)}, f32[4,1280,256]{2,1,0:T(8,128)}) custom-call(bf16[4,8,256,128]{3,2,1,0:T(8,128)(2,1)} %get-tuple-element.76.q_ref, bf16[4,1280,256]{2,1,0:T(8,128)(2,1)} %copy-done, s32[4,1,256]{2,1,0:T(1,128)} %maximum_subtract_fusion.1.low_ref, f32[4,2,2,8,512]{4,3,2,1,0:T(8,128)} %get-tuple-element.82.lse_ref, ...), custom_call_target="tpu_custom_call" | custom-call | tf_op jit(solution)/shard_map/attend_back/pallas_call | solution.py:527
  374.6 2.7 convert.19
  377.5 1.3 collective-permute-start.4
  378.8 1.3 collective-permute-start.7
  380.1 1.3 collective-permute-start.6
  381.4 1.3 collective-permute-start.5
  382.7 12.4 %fusion.8 = (bf16[1,1024,1536]{2,1,0:T(8,128)(2,1)S(1)}, bf16[1,1024,1536]{2,1,0:T(8,128)(2,1)}, bf16[1,1024,1536]{2,1,0:T(8,128)(2,1)}, bf16[1,1024,1536]{2,1,0...) fusion(bf16[6,1024,1536]{2,1,0:T(8,128)(2,1)} %get-tuple-element.92), kind=kLoop, calls=%fused_computation.62 | loop fusion | bytes 37748736 | tf_op jit(solution)/shard_map/unstack | solution.py:882
  395.1 1.4 fusion.5
  396.6 3.7 collective-permute-done.4
  400.3 58.5 %collective-permute-done.7 = bf16[4,256,256]{2,1,0:T(8,128)(2,1)S(1)} collective-permute-done((bf16[4,256,256]{2,1,0:T(8,128)(2,1)S(1)}, bf16[4,256,256]{2,1,0:T(8,128)(2,1)S(1)}, u32[]{:S(2)}, u32[]{:S(2)}) %collective-permute-start.7) | collective-permute-done | bytes 524320 | tf_op jit(solution)/shard_map/ppermute | solution.py:798
  458.9 1.5 convert_add_fusion
  461.2 0.9 pad_maximum_fusion.3.dkv_ref
  462.1 14.5 %finish.1 = (bf16[1024,1280]{1,0:T(8,128)(2,1)}, bf16[1024,1024]{1,0:T(8,128)(2,1)}, f32[8,1024]{1,0:T(8,128)}) custom-call(bf16[1024,1024]{1,0:T(8,128)(2,1)} %bitcast.47, bf16[1024,1024]{1,0:T(8,128)(2,1)} %get-tuple-element.81.h_ref, bf16[4,8,256,128]{3,2,1,0:T(8,128)(2,1)} %get-tuple-element.84.dq_ref, bf16[4,256,256]{2,1,0:T(8,128)(2,1)} %pad_maximum_fusion.3.dkv_ref, ...), custom_call_target="tpu_custom_call" | custom-call | tf_op jit(solution)/shard_map/finish/pallas_call | solution.py:754
  476.5 1.4 fusion.4
  478.0 0.8 copy.48
  478.9 3.7 constant_dynamic-update-slice_fusion.18
  482.6 0.8 constant_dynamic-update-slice_fusion.17
  483.3 1.6 constant_dynamic-update-slice_fusion.16
  484.9 2.1 constant_dynamic-update-slice_fusion.15
  486.9 1.0 copy-done.4
  487.9 2.2 constant_dynamic-update-slice_fusion.14
  490.1 0.9 copy-done.3
  490.9 2.0 constant_dynamic-update-slice_fusion.13
  493.0 1.0 copy-done.2
  494.0 2.1 constant_dynamic-update-slice_fusion.12
  496.0 1.0 copy-done.1
  497.0 2.0 constant_dynamic-update-slice_fusion.11
  499.0 1.9 constant_dynamic-update-slice_fusion.10.own_ref
  500.9 136.9 %scatter_grads.1 = f32[32,11648]{1,0:T(8,128)} custom-call(bf16[2,2,4,2,32,11648]{5,4,3,2,1,0:T(8,128)(2,1)} %constant_dynamic-update-slice_fusion.10.own_ref), custom_call_target="tpu_custom_call" | custom-call | tf_op jit(solution)/shard_map/scatter_grads/pallas_call | solution.py:308
  637.9 1.5 slice_reduce_fusion.3
  639.4 1.3 fusion.10
  640.7 1.7 slice_bitcast_fusion
  642.4 0.9 reshape.321
  643.3 3.1 slice_reduce_fusion
  646.4 1.0 copy.52
  647.4 1.0 copy.51
  648.4 1.0 copy.50
  (67 shorter events, 3.1 us)
Async XLA Ops:
  0.6 43.3 %copy-start.13 = (bf16[32,1024]{1,0:T(8,128)(2,1)S(1)}, bf16[32,1024]{1,0:T(8,128)(2,1)}, u32[]{:S(2)}) copy-start(bf16[32,1024]{1,0:T(8,128)(2,1)} %param.24) | copy-start | bytes 196612
  0.7 43.3 %copy-start.15 = (bf16[32,128]{1,0:T(8,128)(2,1)S(1)}, bf16[32,128]{1,0:T(8,128)(2,1)}, u32[]{:S(2)}) copy-start(bf16[32,128]{1,0:T(8,128)(2,1)} %param.25) | copy-start | bytes 24580
  0.7 43.3 %copy-start.16 = (bf16[32,128]{1,0:T(8,128)(2,1)S(1)}, bf16[32,128]{1,0:T(8,128)(2,1)}, u32[]{:S(2)}) copy-start(bf16[32,128]{1,0:T(8,128)(2,1)} %param.26) | copy-start | bytes 24580
  0.7 43.5 %copy-start.14 = (bf16[1024,32]{0,1:T(8,128)(2,1)S(1)}, bf16[1024,32]{0,1:T(8,128)(2,1)}, u32[]{:S(2)}) copy-start(bf16[1024,32]{0,1:T(8,128)(2,1)} %param.27) | copy-start | bytes 196612
  44.2 0.9 copy-start.11
  173.5 45.7 %collective-permute-start.3 = (bf16[4,256,256]{2,1,0:T(8,128)(2,1)}, bf16[4,256,256]{2,1,0:T(8,128)(2,1)S(1)}, u32[]{:S(2)}, u32[]{:S(2)}) collective-permute-start(bf16[4,256,256]{2,1,0:T(8,128)(2,1)} %get-tuple-element.77), channel_id=1, source_target_pairs={{0,1},{1,2},{2,3},{3,4},{4,5},{5,6},{6,7},{8,9},{9,10},{10,11},{11... | collective-permute-start | bytes 1572872 | tf_op jit(solution)/shard_map/ppermute | solution.py:798
  177.7 41.5 %collective-permute-start.2 = (bf16[4,256,256]{2,1,0:T(8,128)(2,1)}, bf16[4,256,256]{2,1,0:T(8,128)(2,1)S(1)}, u32[]{:S(2)}, u32[]{:S(2)}) collective-permute-start(bf16[4,256,256]{2,1,0:T(8,128)(2,1)} %get-tuple-element.77), channel_id=1, source_target_pairs={{0,2},{1,3},{2,4},{3,5},{4,6},{5,7},{8,10},{9,11},{10,12},{11,13},... | collective-permute-start | bytes 1572872 | tf_op jit(solution)/shard_map/ppermute | solution.py:798
  184.7 34.4 %collective-permute-start.1 = (bf16[4,256,256]{2,1,0:T(8,128)(2,1)}, bf16[4,256,256]{2,1,0:T(8,128)(2,1)S(1)}, u32[]{:S(2)}, u32[]{:S(2)}) collective-permute-start(bf16[4,256,256]{2,1,0:T(8,128)(2,1)} %get-tuple-element.77), channel_id=1, source_target_pairs={{0,3},{1,4},{2,5},{3,6},{4,7},{8,11},{9,12},{10,13},{11,14},{12,15... | collective-permute-start | bytes 1572872 | tf_op jit(solution)/shard_map/ppermute | solution.py:798
  186.1 33.0 %collective-permute-start = (bf16[4,256,256]{2,1,0:T(8,128)(2,1)}, bf16[4,256,256]{2,1,0:T(8,128)(2,1)S(1)}, u32[]{:S(2)}, u32[]{:S(2)}) collective-permute-start(bf16[4,256,256]{2,1,0:T(8,128)(2,1)} %get-tuple-element.77), channel_id=1, source_target_pairs={{0,4},{1,5},{2,6},{3,7},{8,12},{9,13},{10,14},{11,15},{16,20},{17,... | collective-permute-start | bytes 1572872 | tf_op jit(solution)/shard_map/ppermute | solution.py:798
  190.8 28.5 %copy-start.12 = (bf16[4,256,256]{2,1,0:T(8,128)(2,1)S(1)}, bf16[4,256,256]{2,1,0:T(8,128)(2,1)}, u32[]{:S(2)}) copy-start(bf16[4,256,256]{2,1,0:T(8,128)(2,1)} %get-tuple-element.77) | copy-start | bytes 1572868
  219.3 1.6 copy-start
  377.5 22.8 %collective-permute-start.4 = (bf16[4,256,256]{2,1,0:T(8,128)(2,1)S(1)}, bf16[4,256,256]{2,1,0:T(8,128)(2,1)S(1)}, u32[]{:S(2)}, u32[]{:S(2)}) collective-permute-start(bf16[4,256,256]{2,1,0:T(8,128)(2,1)S(1)} %get-tuple-element.104), channel_id=1, source_target_pairs={{1,0},{2,1},{3,2},{4,3},{5,4},{6,5},{7,6},{9,8},{10,9},{11,10},{12... | collective-permute-start | bytes 1572872 | tf_op jit(solution)/shard_map/ppermute | solution.py:798
  378.8 80.0 %collective-permute-start.7 = (bf16[4,256,256]{2,1,0:T(8,128)(2,1)S(1)}, bf16[4,256,256]{2,1,0:T(8,128)(2,1)S(1)}, u32[]{:S(2)}, u32[]{:S(2)}) collective-permute-start(bf16[4,256,256]{2,1,0:T(8,128)(2,1)S(1)} %get-tuple-element.105), channel_id=1, source_target_pairs={{4,0},{5,1},{6,2},{7,3},{12,8},{13,9},{14,10},{15,11},{20,16},{21,... | collective-permute-start | bytes 1572872 | tf_op jit(solution)/shard_map/ppermute | solution.py:798
  380.1 78.7 %collective-permute-start.6 = (bf16[4,256,256]{2,1,0:T(8,128)(2,1)S(1)}, bf16[4,256,256]{2,1,0:T(8,128)(2,1)S(1)}, u32[]{:S(2)}, u32[]{:S(2)}) collective-permute-start(bf16[4,256,256]{2,1,0:T(8,128)(2,1)S(1)} %get-tuple-element.106), channel_id=1, source_target_pairs={{3,0},{4,1},{5,2},{6,3},{7,4},{11,8},{12,9},{13,10},{14,11},{15,12... | collective-permute-start | bytes 1572872 | tf_op jit(solution)/shard_map/ppermute | solution.py:798
  381.4 77.4 %collective-permute-start.5 = (bf16[4,256,256]{2,1,0:T(8,128)(2,1)S(1)}, bf16[4,256,256]{2,1,0:T(8,128)(2,1)S(1)}, u32[]{:S(2)}, u32[]{:S(2)}) collective-permute-start(bf16[4,256,256]{2,1,0:T(8,128)(2,1)S(1)} %get-tuple-element.107), channel_id=1, source_target_pairs={{2,0},{3,1},{4,2},{5,3},{6,4},{7,5},{10,8},{11,9},{12,10},{13,11},... | collective-permute-start | bytes 1572872 | tf_op jit(solution)/shard_map/ppermute | solution.py:798
  396.6 64.1 %copy-start.7 = (f32[4,256,64]{2,1,0:T(8,128)S(1)}, f32[4,256,64]{2,1,0:T(8,128)}, u32[]{:S(2)}) copy-start(f32[4,256,64]{2,1,0:T(8,128)} %get-tuple-element.114) | copy-start | bytes 786436
  396.6 64.2 %copy-start.8 = (f32[4,256,64]{2,1,0:T(8,128)S(1)}, f32[4,256,64]{2,1,0:T(8,128)}, u32[]{:S(2)}) copy-start(f32[4,256,64]{2,1,0:T(8,128)} %get-tuple-element.115) | copy-start | bytes 786436
  396.6 64.2 %copy-start.9 = (f32[4,256,64]{2,1,0:T(8,128)S(1)}, f32[4,256,64]{2,1,0:T(8,128)}, u32[]{:S(2)}) copy-start(f32[4,256,64]{2,1,0:T(8,128)} %get-tuple-element.116) | copy-start | bytes 786436
  478.9 3.7 copy-start.10
  478.9 4.4 copy-start.6
  482.5 2.3 copy-start.5
  484.9 3.0 copy-start.4
  487.9 3.0 copy-start.3
  490.9 3.0 copy-start.2
  494.0 3.0 copy-start.1
  637.8 4.6 slice-start
